TPU v7x, 128 devices: a whole 4x4x4 slice. The times are simulated.
128 devices in a mesh: lat: 8 (over z, core), lon: 16 (over x, y).
Axes of the slice: x: 4, y: 4, z: 4, core: 2. Of those that a mesh axis runs over, the one named last changes fastest.
Arguments:
- runoff: bfloat16 [12, 1024, 4096], P(None, 'lat', 'lon'), may hold values from 0.049804688 to 2
- cell_order: int32 [8, 16, 32768], P('lat', 'lon'), may hold values from 0 to 32767, each once within a row
- map_weights: bfloat16 [8, 16, 256, 128, 128], P('lat', 'lon'), may hold values from 0 to 0.001953125
- dest_device: int32 [8, 16, 256, 1], replicated, may hold values from 0 to 127; in each aligned block of 256 rows (0 to 255, 256 to 511, ..., all dimensions but the last counted through in order) at most 4 rows name the same one
- dest_block: int32 [8, 16, 256], replicated, may hold values from 0 to 127
- initial_flow: float32 [8, 16, 128, 128], P('lat', 'lon'), may hold values from 0.2 to 1
- musk_k: float32 [8, 16, 128, 128], P('lat', 'lon'), may hold values from 2 to 120
- musk_x: float32 [8, 16, 128, 128], P('lat', 'lon'), may hold values from 0 to 0.3
- down_reach: int32 [8, 16, 128, 128], P('lat', 'lon'), may hold values from 1 to 128, as said below
- block_inverse: float32 [8, 16, 128, 128, 128], P('lat', 'lon'), as said below
- upstream_link: int32 [8, 16, 128], P('lat', 'lon'), may hold values from 0 to 127, each once within a row
Outputs:
- discharge: float32 [8, 16, 128, 128], P('lat', 'lon')
Inputs may be any that keep to these rules, and one draw needn't show every extreme that they name: `cell_order`: each row of a device is a permutation of its 32768 cells. `dest_device`: at most 4 source blocks of one device name the same owner, and in every draw some device sends exactly 4 to some owner. `down_reach`: reach i of a block with 0 < i < 127 drains into a reach from i + 1 to 127; reach 0 drains into reach 127, and reach 127 holds 128. block_inverse of a block is the inverse of I - N diag(c1) of that block. `upstream_link`: each device's row is a permutation of its 128 blocks.
All inputs are finite; a program needn't handle non-finite values.
Results may differ from a plain program's by a relative error of at most 0.0003.
Values sent between devices are 32-bit elements; how exact they have to be, the bound alone decides.
No kernel may reach another device: no remote copies, remote signals or barrier semaphores. Data moves between devices by JAX's collectives and lax.ppermute only.
A program may use at most 128 MiB of HBM per device.

v0:
```python
import jax
import jax.numpy as jnp
from jax import lax
from jax.sharding import PartitionSpec as P

substep_seconds = 300.0
highest = lax.Precision.HIGHEST


def passed_along(value, axis, steps):
    count = lax.axis_size(axis)
    initial, last = (max(0, -steps), min(count, count - steps))
    return lax.ppermute(value, axis, [(source, source + steps) for source in range(initial, last)])


def carried_in(array, axis, combine, identity):
    length, index = (lax.axis_size(axis), lax.axis_index(axis))
    everything = jax.tree.map(lambda part: lax.all_gather(part, axis), array)
    start = jax.tree.map(
        lambda part, zero: jnp.broadcast_to(jnp.asarray(zero, part.dtype), part.shape),
        array,
        identity,
    )

    def lap(k, before):
        reached = k < index
        new = combine(before, jax.tree.map(lambda part: part[k], everything))
        return jax.tree.map(lambda a, b: jnp.where(reached, a, b), new, before)

    return lax.fori_loop(0, length, lap, start)


def coefficients(travel, weighting):
    half = 0.5 * substep_seconds
    denom = travel * (1.0 - weighting) + half
    first = (half - travel * weighting) / denom
    second = (half + travel * weighting) / denom
    third = (travel * (1.0 - weighting) - half) / denom
    return (first, second, third)


def chain_step(earlier, later):
    early_out, early_gain, early_link = earlier
    late_out, late_gain, late_link = later
    chosen = late_link[:, None] == jnp.arange(late_out.shape[0], dtype=jnp.float32)[None, :]

    def select(values):
        return jnp.sum(jnp.where(chosen, values[None, :], 0.0), axis=1)

    return (
        late_out + late_gain * select(early_out),
        late_gain * select(early_gain),
        select(early_link),
    )


def body(
    runoff,
    cell_order,
    map_weights,
    dest_device,
    dest_block,
    initial_flow,
    musk_k,
    musk_x,
    down_reach,
    block_inverse,
    upstream_link,
):
    steps = runoff.shape[0]
    lat_count = lax.axis_size("lat")
    lon_count = lax.axis_size("lon")
    devices = lat_count * lon_count
    my_index = lax.axis_index("lat") * lon_count + lax.axis_index("lon")
    weights = map_weights.reshape(map_weights.shape[2:])
    sources, cell_block, reaches = weights.shape
    slots = max(2, 2 * sources // devices)
    cell_rows = runoff.reshape(steps, -1).T
    picked = jnp.take(cell_rows, cell_order.reshape(-1), axis=0).reshape(sources, cell_block, steps)
    contrib = lax.dot_general(
        picked, weights, (((1,), (1,)), ((0,), (0,))), preferred_element_type=jnp.float32
    )
    targets = dest_device.reshape(devices, sources)
    target_blocks = dest_block.reshape(devices, sources)
    my_targets = lax.dynamic_index_in_dim(targets, my_index, 0, keepdims=False)
    peers = jnp.arange(devices, dtype=jnp.int32)
    marks = (my_targets[:, None] == peers[None, :]).astype(jnp.int32)
    ranks = jnp.sum((jnp.cumsum(marks, axis=0) - 1) * marks, axis=1)
    slot_ids = my_targets * slots + ranks
    placing = (jnp.arange(devices * slots, dtype=jnp.int32)[:, None] == slot_ids[None, :]).astype(
        jnp.float32
    )
    outgoing = jnp.dot(placing, contrib.reshape(sources, steps * reaches), precision=highest)
    outgoing = outgoing.reshape(devices, slots, steps, reaches)
    arrived = lax.all_to_all(outgoing, ("lat", "lon"), split_axis=0, concat_axis=0, tiled=True)
    arrived = arrived.reshape(devices * slots, steps * reaches)
    blocks = initial_flow.shape[2]
    hits = targets == my_index
    positions = jnp.where(hits, jnp.cumsum(hits.astype(jnp.int32), axis=1) - 1, slots)
    slot_match = positions[:, :, None] == jnp.arange(slots, dtype=jnp.int32)[None, None, :]
    filled = jnp.sum(slot_match.astype(jnp.int32), axis=1)
    named = jnp.sum(jnp.where(slot_match, target_blocks[:, :, None], 0), axis=1)
    slot_block = jnp.where(filled > 0, named, blocks)
    selector = (
        slot_block.reshape(-1)[None, :] == jnp.arange(blocks, dtype=jnp.int32)[:, None]
    ).astype(jnp.float32)
    lateral = jnp.dot(selector, arrived, precision=highest).reshape(blocks, steps, reaches)
    flow = initial_flow.reshape(blocks, reaches)
    first, second, third = coefficients(
        musk_k.reshape(blocks, reaches), musk_x.reshape(blocks, reaches)
    )
    inverse = block_inverse.reshape(blocks, reaches, reaches)
    drains = down_reach.reshape(blocks, reaches)
    upstream_matrix = (
        drains[:, None, :] == jnp.arange(reaches, dtype=jnp.int32)[None, :, None]
    ).astype(jnp.float32)
    head_gain = first[:, 0:1] * inverse[:, :, 0]
    outlet_gain = head_gain[:, reaches - 1]
    links = upstream_link.reshape(blocks)
    link_values = links.astype(jnp.float32)
    link_select = (links[:, None] == jnp.arange(blocks, dtype=jnp.int32)[None, :]).astype(
        jnp.float32
    )
    start = passed_along(flow[:, reaches - 1], "lon", 1)
    inflow_prev = jnp.dot(link_select, start, precision=highest)
    identity = (
        jnp.zeros((blocks,), jnp.float32),
        jnp.ones((blocks,), jnp.float32),
        jnp.arange(blocks, dtype=jnp.float32),
    )
    for step in range(steps):
        known = (
            (first + second) * lateral[:, step, :]
            + second * jnp.einsum("bji,bi->bj", upstream_matrix, flow, precision=highest)
            + third * flow
        )
        known = known.at[:, 0].add(second[:, 0] * inflow_prev)
        local = jnp.einsum("brs,bs->br", inverse, known, precision=highest)
        prefix = carried_in(
            (local[:, reaches - 1], outlet_gain, link_values), "lon", chain_step, identity
        )
        inflow_prev = jnp.dot(link_select, prefix[0], precision=highest)
        flow = local + head_gain * inflow_prev[:, None]
    return flow.reshape(initial_flow.shape)


def solution(mesh):
    return jax.shard_map(
        body,
        mesh=mesh,
        in_specs=(
            P(None, "lat", "lon"),
            P("lat", "lon", None),
            P("lat", "lon", None, None, None),
            P(),
            P(),
            P("lat", "lon", None, None),
            P("lat", "lon", None, None),
            P("lat", "lon", None, None),
            P("lat", "lon", None, None),
            P("lat", "lon", None, None, None),
            P("lat", "lon", None),
        ),
        out_specs=P("lat", "lon", None, None),
        check_vma=False,
    )
```

profile of v0, /device:TPU:0, one launch (start us, length us, event | category | flops | bytes accessed | tf_op | source)
XLA Modules:
  0.0 637.3 jit_solution(7493398831439783876)
XLA Ops:
  1.6 7.6 %copy.94 = bf16[12,128,256]{0,2,1:T(8,128)(2,1)} copy(bf16[12,128,256]{2,1,0:T(8,128)(2,1)} %param.59) | data formatting | bytes 1572864 | tf_op args[0]
  9.4 113.8 %gather_fusion = bf16[32768,12]{1,0:T(8,128)(2,1)} fusion(bf16[32768,12]{1,0:T(8,128)(2,1)} %bitcast.683, s32[32768]{0:T(1024)S(1)} %broadcast_clamp_fusion), kind=kCustom, calls=%fused_computation | custom fusion | bytes 1703936 | tf_op jit(solution)/shard_map/jit(_take)/gather | solution.py:79
  123.2 7.3 %copy.95 = bf16[256,128,12]{1,2,0:T(8,128)(2,1)S(1)} copy(bf16[256,128,12]{2,1,0:T(8,128)(2,1)} %bitcast.684) | data formatting | bytes 1572864 | tf_op jit(solution)/shard_map/jit(_take)/gather | solution.py:79
  130.5 4.7 fusion.60
  143.5 11.2 %all-to-all-start = ((f32[128,4,12,128]{3,1,2,0:T(4,128)}), f32[128,4,12,128]{3,1,2,0:T(4,128)S(1)}, u32[]{:S(2)}, u32[]{:S(2)}) async-start(f32[128,4,12,128]{3,1,2,0:T(4,128)} %copy.97), calls=%async_computation | async-start | bytes 6291456 | tf_op jit(solution)/shard_map/all_to_all | solution.py:95
  175.7 9.4 %copy.101 = f32[1,1,128,128,128]{2,3,4,1,0:T(8,128)} copy(f32[1,1,128,128,128]{4,3,2,1,0:T(8,128)} %param.68) | data formatting | bytes 16777216 | tf_op args[9]
  185.1 9.3 %copy.112 = f32[128,128,128]{0,2,1:T(8,128)} copy(f32[128,128,128]{1,2,0:T(8,128)} %bitcast.685) | data formatting | bytes 16777216
  195.1 19.7 %all-gather.2 = f32[16,1,128]{2,1,0:T(1,128)S(1)} all-gather(f32[1,1,128]{2,1,0:T(1,128)S(1)} %convert_element_type.36), channel_id=4, replica_groups=mesh['lat'=8,'lon'=16] {'lon'}, dimensions={0}, use_global_device_ids=true | all-gather | bytes 8704 | tf_op jit(solution)/shard_map/all_gather | solution.py:18
  223.7 19.3 %all-gather.1 = f32[2048,1]{0,1:T(1,128)S(1)} all-gather(f32[128,1]{0,1:T(1,128)S(1)} %slice.381), channel_id=3, replica_groups=mesh['lat'=8,'lon'=16] {'lon'}, dimensions={0}, use_global_device_ids=true | all-gather | bytes 8704 | tf_op jit(solution)/shard_map/all_gather | solution.py:18
  244.6 4.2 multiply_reduce_fusion.11
  248.8 19.5 %all-gather = f32[2048,1]{0,1:T(1,128)S(1)} all-gather(f32[128,1]{0,1:T(1,128)S(1)} %slice.380), channel_id=2, replica_groups=mesh['lat'=8,'lon'=16] {'lon'}, dimensions={0}, use_global_device_ids=true | all-gather | bytes 8704 | tf_op jit(solution)/shard_map/all_gather | solution.py:18
  277.7 4.2 multiply_reduce_fusion.10
  281.9 19.3 %all-gather.3 = f32[2048,1]{0,1:T(1,128)S(1)} all-gather(f32[128,1]{0,1:T(1,128)S(1)} %slice.383), channel_id=5, replica_groups=mesh['lat'=8,'lon'=16] {'lon'}, dimensions={0}, use_global_device_ids=true | all-gather | bytes 8704 | tf_op jit(solution)/shard_map/all_gather | solution.py:18
  310.6 4.2 multiply_reduce_fusion.9
  314.8 19.5 %all-gather.4 = f32[2048,1]{0,1:T(1,128)S(1)} all-gather(f32[128,1]{0,1:T(1,128)S(1)} %slice.385), channel_id=6, replica_groups=mesh['lat'=8,'lon'=16] {'lon'}, dimensions={0}, use_global_device_ids=true | all-gather | bytes 8704 | tf_op jit(solution)/shard_map/all_gather | solution.py:18
  343.6 4.2 multiply_reduce_fusion.8
  347.9 19.3 %all-gather.5 = f32[2048,1]{0,1:T(1,128)S(1)} all-gather(f32[128,1]{0,1:T(1,128)S(1)} %slice.387), channel_id=7, replica_groups=mesh['lat'=8,'lon'=16] {'lon'}, dimensions={0}, use_global_device_ids=true | all-gather | bytes 8704 | tf_op jit(solution)/shard_map/all_gather | solution.py:18
  376.6 4.2 multiply_reduce_fusion.7
  380.8 19.7 %all-gather.6 = f32[2048,1]{0,1:T(1,128)S(1)} all-gather(f32[128,1]{0,1:T(1,128)S(1)} %slice.389), channel_id=8, replica_groups=mesh['lat'=8,'lon'=16] {'lon'}, dimensions={0}, use_global_device_ids=true | all-gather | bytes 8704 | tf_op jit(solution)/shard_map/all_gather | solution.py:18
  409.9 4.2 multiply_reduce_fusion.6
  414.1 19.3 %all-gather.7 = f32[2048,1]{0,1:T(1,128)S(1)} all-gather(f32[128,1]{0,1:T(1,128)S(1)} %slice.391), channel_id=9, replica_groups=mesh['lat'=8,'lon'=16] {'lon'}, dimensions={0}, use_global_device_ids=true | all-gather | bytes 8704 | tf_op jit(solution)/shard_map/all_gather | solution.py:18
  442.8 4.2 multiply_reduce_fusion.5
  447.0 19.4 %all-gather.8 = f32[2048,1]{0,1:T(1,128)S(1)} all-gather(f32[128,1]{0,1:T(1,128)S(1)} %slice.393), channel_id=10, replica_groups=mesh['lat'=8,'lon'=16] {'lon'}, dimensions={0}, use_global_device_ids=true | all-gather | bytes 8704 | tf_op jit(solution)/shard_map/all_gather | solution.py:18
  475.8 4.2 multiply_reduce_fusion.4
  480.0 19.3 %all-gather.9 = f32[2048,1]{0,1:T(1,128)S(1)} all-gather(f32[128,1]{0,1:T(1,128)S(1)} %slice.395), channel_id=11, replica_groups=mesh['lat'=8,'lon'=16] {'lon'}, dimensions={0}, use_global_device_ids=true | all-gather | bytes 8704 | tf_op jit(solution)/shard_map/all_gather | solution.py:18
  508.7 4.2 multiply_reduce_fusion.3
  512.9 19.5 %all-gather.10 = f32[2048,1]{0,1:T(1,128)S(1)} all-gather(f32[128,1]{0,1:T(1,128)S(1)} %slice.397), channel_id=12, replica_groups=mesh['lat'=8,'lon'=16] {'lon'}, dimensions={0}, use_global_device_ids=true | all-gather | bytes 8704 | tf_op jit(solution)/shard_map/all_gather | solution.py:18
  541.8 4.2 multiply_reduce_fusion.2
  546.0 19.3 %all-gather.11 = f32[2048,1]{0,1:T(1,128)S(1)} all-gather(f32[128,1]{0,1:T(1,128)S(1)} %slice.399), channel_id=13, replica_groups=mesh['lat'=8,'lon'=16] {'lon'}, dimensions={0}, use_global_device_ids=true | all-gather | bytes 8704 | tf_op jit(solution)/shard_map/all_gather | solution.py:18
  574.7 4.2 multiply_reduce_fusion.1
  578.9 19.5 %all-gather.12 = f32[2048,1]{0,1:T(1,128)S(1)} all-gather(f32[128,1]{0,1:T(1,128)S(1)} %slice.401), channel_id=14, replica_groups=mesh['lat'=8,'lon'=16] {'lon'}, dimensions={0}, use_global_device_ids=true | all-gather | bytes 8704 | tf_op jit(solution)/shard_map/all_gather | solution.py:18
  612.0 19.3 %all-gather.13 = f32[2048,1]{0,1:T(1,128)S(1)} all-gather(f32[128,1]{0,1:T(1,128)S(1)} %slice.403), channel_id=15, replica_groups=mesh['lat'=8,'lon'=16] {'lon'}, dimensions={0}, use_global_device_ids=true | all-gather | bytes 8704 | tf_op jit(solution)/shard_map/all_gather | solution.py:18
  (979 shorter events, 194.4 us)
Async XLA Ops:
  0.0 9.3 %copy-start.1 = (s32[1,1,32768]{2,1,0:T(1,128)S(1)}, s32[1,1,32768]{2,1,0:T(1,128)}, u32[]{:S(2)}) copy-start(s32[1,1,32768]{2,1,0:T(1,128)} %param.60) | copy-start | bytes 393220
  136.9 17.8 %copy-start.3 = (f32[1,1,128,128]{3,2,1,0:T(8,128)S(1)}, f32[1,1,128,128]{3,2,1,0:T(8,128)}, u32[]{:S(2)}) copy-start(f32[1,1,128,128]{3,2,1,0:T(8,128)} %param.64) | copy-start | bytes 196612
  136.9 23.8 %copy-start.2 = (s32[8,16,256,1]{2,3,1,0:T(1,128)S(1)}, s32[8,16,256,1]{2,3,1,0:T(1,128)}, u32[]{:S(2)}) copy-start(s32[8,16,256,1]{2,3,1,0:T(1,128)} %param.62) | copy-start | bytes 393220
  139.8 30.5 %copy-start = (s32[1,1,128,128]{3,2,1,0:T(8,128)S(1)}, s32[1,1,128,128]{3,2,1,0:T(8,128)}, u32[]{:S(2)}) copy-start(s32[1,1,128,128]{3,2,1,0:T(8,128)} %param.67) | copy-start | bytes 196612
  143.5 71.3 %all-to-all-start = ((f32[128,4,12,128]{3,1,2,0:T(4,128)}), f32[128,4,12,128]{3,1,2,0:T(4,128)S(1)}, u32[]{:S(2)}, u32[]{:S(2)}) async-start(f32[128,4,12,128]{3,1,2,0:T(4,128)} %copy.97), calls=%async_computation | async-start | bytes 6291456 | tf_op jit(solution)/shard_map/all_to_all | solution.py:95
  156.6 86.3 %collective-permute-start = (f32[128]{0:T(128)}, f32[128]{0:T(128)}, u32[]{:S(2)}, u32[]{:S(2)}) collective-permute-start(f32[128]{0:T(128)} %slice_bitcast_fusion.16), channel_id=1, source_target_pairs={{0,1},{1,2},{2,3},{3,4},{4,5},{5,6},{6,7},{7,8},{8,9},{9,10},{10,1... | collective-permute-start | bytes 1544 | tf_op jit(solution)/shard_map/ppermute | solution.py:13
  185.1 9.3 %copy-start.14 = (s32[1,1,128]{2,1,0:T(1,128)S(1)}, s32[1,1,128]{2,1,0:T(1,128)}, u32[]{:S(2)}) copy-start(s32[1,1,128]{2,1,0:T(1,128)} %param.69) | copy-start | bytes 1540
  215.4 3.9 copy-start.13
  215.4 7.3 %copy-start.4 = (f32[128,128]{0,1:T(8,128)S(1)}, f32[128,128]{0,1:T(8,128)}, u32[]{:S(2)}) copy-start(f32[128,128]{0,1:T(8,128)} %copy.237) | copy-start | bytes 196612
  216.9 51.4 %copy-start.12 = (f32[128]{0:T(128)S(1)}, f32[128]{0:T(128)}, u32[]{:S(2)}) copy-start(f32[128]{0:T(128)} %custom-call) | copy-start | bytes 1540
  244.6 56.6 %copy-start.11 = (f32[128]{0:T(128)S(1)}, f32[128]{0:T(128)}, u32[]{:S(2)}) copy-start(f32[128]{0:T(128)} %custom-call.1) | copy-start | bytes 1540
  277.7 56.6 %copy-start.10 = (f32[128]{0:T(128)S(1)}, f32[128]{0:T(128)}, u32[]{:S(2)}) copy-start(f32[128]{0:T(128)} %custom-call.2) | copy-start | bytes 1540
  310.6 56.6 %copy-start.9 = (f32[128]{0:T(128)S(1)}, f32[128]{0:T(128)}, u32[]{:S(2)}) copy-start(f32[128]{0:T(128)} %custom-call.3) | copy-start | bytes 1540
  343.6 56.9 %copy-start.8 = (f32[128]{0:T(128)S(1)}, f32[128]{0:T(128)}, u32[]{:S(2)}) copy-start(f32[128]{0:T(128)} %custom-call.4) | copy-start | bytes 1540
  376.6 56.8 %copy-start.7 = (f32[128]{0:T(128)S(1)}, f32[128]{0:T(128)}, u32[]{:S(2)}) copy-start(f32[128]{0:T(128)} %custom-call.5) | copy-start | bytes 1540
  409.9 56.5 %copy-start.6 = (f32[128]{0:T(128)S(1)}, f32[128]{0:T(128)}, u32[]{:S(2)}) copy-start(f32[128]{0:T(128)} %custom-call.6) | copy-start | bytes 1540
  442.8 56.5 %copy-start.5 = (f32[128]{0:T(128)S(1)}, f32[128]{0:T(128)}, u32[]{:S(2)}) copy-start(f32[128]{0:T(128)} %custom-call.7) | copy-start | bytes 1540
where the time goes:
time: 646 us; the launch traced here: 637 us
  blocking collectives  272 us (42%)
  local copies, waits for them, and re-layouts  173 us (27%)
  other arithmetic  153 us (24%)
  starting transfers between devices  15.1 us (2%)
  matrix products  14.9 us (2%)
  loops' own time  7.93 us (1%)
    all_gather x14, blocking collectives, carried_in(): everything = jax.tree.map(lambda part: lax.all_gather(part, axis), array)  272 us
    gather x2, local copies, waits for them, and re-layouts, body(): jnp.take(cell_rows, cell_order.reshape(-1), axis=0)  121 us
    dot_general x12, other arithmetic, body(): local = jnp.einsum('brs,bs->br', inverse, known, precision=highest)  50.4 us
    unnamed x24, other arithmetic  40.3 us
    reduce_sum x192, other arithmetic, select(): return jnp.sum(jnp.where(chosen, values[None, :], 0.0), axis=1)  32.6 us
    unnamed x49, local copies, waits for them, and re-layouts  32.4 us
  transfers between devices with their start and end apart: 2, of which 0 were waited for; matrix products, arithmetic and copies ran while one was open for 7% of the time, Pallas kernels for 0%

commit v1 on v0

v1 whole, which is shorter than its diff:
```python
import functools
import jax
import jax.numpy as jnp
from jax import lax
from jax.experimental import pallas as pl
from jax.experimental.pallas import tpu as pltpu
from jax.sharding import PartitionSpec as P

substep_seconds = 300.0

VREGS = 32
CHUNKS = 4

def gathered(x, index, axis):
    return jnp.take_along_axis(x, index, axis=axis, mode="promise_in_bounds")

def map_kernel(slots, order_ref, runoff_ref, target_ref, weights_ref, out_ref,
               pick_ref, held_ref, marks_ref, subs_ref, lanes_ref, counts_ref, sems):
    sources = weights_ref.shape[0]
    part = sources // CHUNKS
    def fetch(i):
        rows = pl.ds(i * part, part)
        return pltpu.make_async_copy(weights_ref.at[rows], held_ref.at[rows], sems.at[i])
    for i in range(CHUNKS):
        fetch(i).start()

    lane = lax.broadcasted_iota(jnp.int32, (8, 128), 1)
    sub = lax.broadcasted_iota(jnp.int32, (8, 128), 0)
    keys = []
    for v in range(VREGS):
        c = order_ref[pl.ds(8 * v, 8), :]
        keys.append(((c & 127) << 8) | (((c >> 8) & 7) << 5) | (((c >> 7) & 1) << 4) | (c >> 11))

    def flips(q):
        if q == 0 or q >= 15:
            return [None] * VREGS
        if q < 5:
            return [bool((v >> q) & 1) for v in range(VREGS)]
        bit = (sub >> (q - 5)) & 1 if q < 8 else (lane >> (q - 8)) & 1
        return [bit] * VREGS

    def as_word(flip):
        if flip is None or flip is False:
            return None
        if flip is True:
            return -1
        return -flip

    pair = 0
    undo = []
    for q in range(1, 16):
        before, now = flips(q - 1), flips(q)
        for v in range(VREGS):
            a, b = as_word(before[v]), as_word(now[v])
            if a is None and b is None:
                continue
            if isinstance(a, int) and isinstance(b, int):
                continue
            word = b if a is None else (a if b is None else a ^ b)
            keys[v] = keys[v] ^ word
        lane_bits = [k for k in range(q - 1, 7, -1)]
        sub_bits = [k for k in range(min(q - 1, 7), 4, -1)]
        for bits, axis, place, low, ref in ((lane_bits, 1, lane, 8, lanes_ref), (sub_bits, 0, sub, 5, subs_ref)):
            if not bits:
                continue
            marks = [[] for _ in range(VREGS)]
            for k in bits:
                d = 1 << (k - low)
                partner = place ^ d
                upper = (place & d) != 0
                for v in range(VREGS):
                    other = gathered(keys[v], partner, axis)
                    new = jnp.where(upper, jnp.maximum(keys[v], other), jnp.minimum(keys[v], other))
                    marks[v].append((new != keys[v], partner))
                    keys[v] = new
            row = (q - 9) if axis == 1 else (q - 6)
            for v in range(VREGS):
                index = place
                for mark, partner in reversed(marks[v]):
                    other = partner if index is place else gathered(index, partner, axis)
                    index = jnp.where(mark, other, index)
                ref[row * VREGS + v] = index
        pairs = []
        for k in range(min(q - 1, 4), -1, -1):
            for v in range(VREGS):
                if v & (1 << k):
                    continue
                w = v | (1 << k)
                a, b = keys[v], keys[w]
                marks_ref[pair] = (a > b).astype(jnp.int32)
                keys[v], keys[w] = jnp.minimum(a, b), jnp.maximum(a, b)
                pairs.append((pair, v, w))
                pair += 1
        undo.append((q, pairs))

    planes = runoff_ref.shape[0] // 2

    def plane(p, carry):
        low = (runoff_ref[p].astype(jnp.float32) * 4096.0).astype(jnp.int32)
        high = (runoff_ref[p + planes].astype(jnp.float32) * 4096.0).astype(jnp.int32)
        both = low | (high << 16)
        x = []
        for h in range(2):
            for r in range(16):
                x.append(both[8 * r:8 * r + 8, 128 * h:128 * h + 128])
        for q, pairs in reversed(undo):
            for at, v, w in reversed(pairs):
                mark = marks_ref[at] != 0
                x[v], x[w] = jnp.where(mark, x[w], x[v]), jnp.where(mark, x[v], x[w])
            if q >= 6:
                for v in range(VREGS):
                    x[v] = gathered(x[v], subs_ref[(q - 6) * VREGS + v], 0)
            if q >= 9:
                for v in range(VREGS):
                    x[v] = gathered(x[v], lanes_ref[(q - 9) * VREGS + v], 1)
        scale = 1.0 / 4096.0
        for v in range(VREGS):
            pick_ref[pl.ds(128 * v + p, 8, stride=16), :] = (x[v] & 0xFFFF).astype(jnp.float32) * scale
            pick_ref[pl.ds(128 * v + p + planes, 8, stride=16), :] = (x[v] >> 16).astype(jnp.float32) * scale
        return carry

    lax.fori_loop(0, planes, plane, 0)

    out_ref[...] = jnp.zeros_like(out_ref)
    def clear(d, carry):
        counts_ref[d] = 0
        return carry
    lax.fori_loop(0, counts_ref.shape[0], clear, 0)
    steps = 2 * planes
    unroll = 8
    for i in range(CHUNKS):
        fetch(i).wait()
        def group(g, carry):
            for u in range(unroll):
                s = i * part + g * unroll + u
                lhs = pick_ref[pl.ds(pl.multiple_of(s * 16, 16), 16), :].astype(jnp.bfloat16)
                c = jnp.dot(lhs, held_ref[s], preferred_element_type=jnp.float32)
                d = target_ref[s]
                k = counts_ref[d]
                counts_ref[d] = k + 1
                out_ref[pl.ds(d * (slots * steps) + k, steps, stride=slots), :] = c[:steps]
            return carry
        lax.fori_loop(0, part // unroll, group, 0)


def map_sources(order, runoff, target, weights, devices, slots):
    steps = runoff.shape[0]
    sources, cells, reaches = weights.shape
    vmem = pl.BlockSpec(memory_space=pltpu.VMEM)
    return pl.pallas_call(
        functools.partial(map_kernel, slots),
        out_shape=jax.ShapeDtypeStruct((devices * slots * steps, reaches), jnp.float32),
        in_specs=[vmem, vmem, pl.BlockSpec(memory_space=pltpu.SMEM), pl.BlockSpec(memory_space=pl.ANY)],
        out_specs=vmem,
        scratch_shapes=[
            pltpu.VMEM((sources * 16, cells), jnp.float32),
            pltpu.VMEM(weights.shape, weights.dtype),
            pltpu.VMEM((1040, 8, 128), jnp.int32),
            pltpu.VMEM((10 * VREGS, 8, 128), jnp.int32),
            pltpu.VMEM((7 * VREGS, 8, 128), jnp.int32),
            pltpu.SMEM((devices,), jnp.int32),
            pltpu.SemaphoreType.DMA((CHUNKS,)),
        ],
        compiler_params=pltpu.CompilerParams(vmem_limit_bytes=56 * 1024 * 1024),
    )(order, runoff, target, weights)


def coefficients(travel, weighting):
    half = 0.5 * substep_seconds
    denom = travel * (1.0 - weighting) + half
    first = (half - travel * weighting) / denom
    second = (half + travel * weighting) / denom
    third = (travel * (1.0 - weighting) - half) / denom
    return first, second, third


TILES = 16
SIZE = 128


def prepare_kernel(steps, slots, inverse_ref, travel_ref, weighting_ref, drains_ref, flow_ref, links_ref,
                   targets_ref, blocks_ref, me_ref, spread_ref, rows_ref, heads_ref, terms_ref, note_ref,
                   select_ref, left_ref, scaled_ref, product_ref):
    first, second, third = coefficients(travel_ref[...], weighting_ref[...])
    drains = drains_ref[...]
    nearest = jnp.minimum(drains, SIZE - 1)
    below = jnp.concatenate(
        [gathered(second[8 * i:8 * i + 8], nearest[8 * i:8 * i + 8], 1) for i in range(TILES)], axis=0)
    below = jnp.where(drains < SIZE, below, 0.0)
    ratio = below / first
    terms_ref[0] = (ratio + third).T
    terms_ref[1] = ratio.T
    terms_ref[2] = (first + second).T
    terms_ref[3] = flow_ref[...].T
    note_ref[...] = jnp.zeros_like(note_ref)
    note_ref[0:1, :] = terms_ref[3, SIZE - 1:SIZE, :]
    note_ref[13:14, :] = first.T[0:1, :]
    note_ref[14:15, :] = second.T[0:1, :]
    note_ref[15:16, :] = links_ref[...].astype(jnp.float32)

    hits = targets_ref[...] == me_ref[0]
    sources = hits.shape[1]
    order = lax.broadcasted_iota(jnp.int32, (sources, sources), 0)
    later = (order <= lax.broadcasted_iota(jnp.int32, (sources, sources), 1)).astype(jnp.bfloat16)
    place = jnp.dot(hits.astype(jnp.bfloat16), later, preferred_element_type=jnp.float32)
    column = lax.broadcasted_iota(jnp.int32, (SIZE, SIZE), 1).astype(jnp.float32)
    numbers = blocks_ref[...].astype(jnp.float32) + 1.0
    for k in range(slots):
        here = hits & (place == k + 1.0)
        named = jnp.sum(jnp.where(here, numbers, 0.0), axis=1, keepdims=True) - 1.0
        select_ref[k] = (named == column).astype(jnp.float32).T.astype(jnp.bfloat16)

    def turned(g, carry):
        for u in range(4):
            r = g * 4 + u
            spread_ref[pl.ds(r, SIZE, stride=SIZE), :] = inverse_ref[pl.ds(r, SIZE, stride=SIZE), :].T
        return carry

    lax.fori_loop(0, SIZE // 4, turned, 0)

    left_ref[...] = (lax.broadcasted_iota(jnp.int32, (SIZE, SIZE), 0) == SIZE - 1).astype(jnp.float32)
    heads_ref[0] = spread_ref[0:SIZE, :]

    def power(k, carry):
        head = heads_ref[k]
        scaled_ref[...] = terms_ref[0] * head
        left = [left_ref[8 * i:8 * i + 8, :] for i in range(TILES)]
        sums = [jnp.zeros((8, SIZE), jnp.float32) for _ in range(TILES)]
        for s in range(SIZE):
            factor = scaled_ref[s:s + 1, :]
            total = None
            for i in range(s // 8, TILES):
                part = spread_ref[s * SIZE + 8 * i:s * SIZE + 8 * i + 8, :]
                sums[i] = sums[i] + part * factor
                term = part * left[i]
                total = term if total is None else total + term
            product_ref[s:s + 1, :] = jnp.sum(total, axis=0, keepdims=True)
        after = jnp.minimum(k + 1, steps - 1)
        heads = jnp.concatenate(sums, axis=0) - terms_ref[1] * head
        @pl.when(k < steps - 1)
        def _():
            heads_ref[after] = heads
        product = product_ref[...]
        rows_ref[k] = product * terms_ref[2]
        note_ref[pl.ds(16 + k, 1), :] = product[0:1, :]
        new = product * terms_ref[0] - left_ref[...] * terms_ref[1]
        left_ref[...] = new
        note_ref[pl.ds(1 + k, 1), :] = jnp.sum(new * terms_ref[3], axis=0, keepdims=True)
        return carry

    lax.fori_loop(0, steps, power, 0)


def lateral_kernel(steps, slots, arrived_ref, select_ref, rows_ref, note_ref, lateral_ref, notes_ref):
    sources = arrived_ref.shape[0] // (slots * steps)
    for t in range(steps):
        total = None
        for k in range(slots):
            piece = arrived_ref[pl.ds(t * slots + k, sources, stride=slots * steps), :]
            high = piece.astype(jnp.bfloat16)
            low = (piece - high.astype(jnp.float32)).astype(jnp.bfloat16)
            for part in (high, low):
                term = jnp.dot(select_ref[k], part, preferred_element_type=jnp.float32)
                total = term if total is None else total + term
        lateral_ref[t] = total.T
    sums = [jnp.zeros((8, SIZE), jnp.float32) for _ in range(steps)]
    for i in range(TILES):
        tile = slice(8 * i, 8 * i + 8)
        given = [lateral_ref[t, tile, :] for t in range(steps)]
        weight = [rows_ref[t, tile, :] for t in range(steps)]
        for t in range(steps):
            for j in range(t + 1):
                sums[t] = sums[t] + weight[t - j] * given[j]
    note = note_ref[...]
    series = [jnp.sum(part, axis=0, keepdims=True) for part in sums]
    whole = jnp.concatenate(
        [note[0:1]] + [note[1 + t:2 + t] + series[t] for t in range(steps)] + [note[1 + steps:]], axis=0)
    for d in range(notes_ref.shape[0]):
        notes_ref[d] = whole


def local_kernel(steps, spread_ref, terms_ref, lateral_ref, flow_ref, scaled_ref, held_ref, sems):
    def fetch(i):
        rows = pl.ds(i * 2048, 2048)
        return pltpu.make_async_copy(spread_ref.at[rows], held_ref.at[rows], sems.at[i])

    for i in range(8):
        fetch(i).start()
    flow_ref[...] = terms_ref[3]

    def step(t, wait):
        flow = flow_ref[...]
        scaled_ref[...] = terms_ref[0] * flow + terms_ref[2] * lateral_ref[t]
        sums = [jnp.zeros((8, SIZE), jnp.float32) for _ in range(TILES)]
        for s in range(SIZE):
            if wait and s % 16 == 0:
                fetch(s // 16).wait()
            factor = scaled_ref[s:s + 1, :]
            for i in range(s // 8, TILES):
                sums[i] = sums[i] + held_ref[s * SIZE + 8 * i:s * SIZE + 8 * i + 8, :] * factor
        flow_ref[...] = jnp.concatenate(sums, axis=0) - terms_ref[1] * flow

    step(0, True)

    def rest(t, carry):
        step(t, False)
        return carry

    lax.fori_loop(1, steps, rest, 0)


def chain_kernel(steps, notes_ref, flow_ref, heads_ref, lon_ref, out_ref, pad_ref):
    count = notes_ref.shape[0]
    me = lon_ref[0]
    row = lax.broadcasted_iota(jnp.int32, (16, SIZE), 0)
    zeros = jnp.zeros((16, SIZE), jnp.float32)
    for k in range(count):
        pad_ref[k, 0:16, :] = zeros
        pad_ref[k, 16:32, :] = notes_ref[k, 16:32, :]

    def inlet(k, series):
        link = jnp.broadcast_to(notes_ref[k, 15:16, :].astype(jnp.int32), (16, SIZE))
        coming = jnp.concatenate([gathered(series[0:8], link[0:8], 1), gathered(series[8:16], link[0:8], 1)], axis=0)
        coming = jnp.where(row <= steps, coming, 0.0)
        return notes_ref[k, 13:14, :] * coming + notes_ref[k, 14:15, :] * pltpu.roll(coming, 1, 0)

    def hop(k, series):
        entering = inlet(k, series)
        new = notes_ref[k, 0:16, :]
        for t in range(1, steps + 1):
            new = new + pad_ref[k, 16 - t:32 - t, :] * entering[t:t + 1, :]
        return new

    series = lax.fori_loop(1, me, hop, notes_ref[0, 0:16, :])
    entering = jnp.where(me > 0, inlet(me, series), 0.0)
    flow = flow_ref[...]
    for t in range(1, steps + 1):
        flow = flow + heads_ref[steps - t] * entering[t:t + 1, :]
    out_ref[...] = flow.T


def body(runoff, cell_order, map_weights, dest_device, dest_block, initial_flow, musk_k, musk_x, down_reach,
         block_inverse, upstream_link):
    steps = runoff.shape[0]
    lat_count, lon_count = lax.axis_size("lat"), lax.axis_size("lon")
    devices = lat_count * lon_count
    lon_index = lax.axis_index("lon")
    my_index = lax.axis_index("lat") * lon_count + lon_index
    weights = map_weights.reshape(map_weights.shape[2:])
    sources, cells, reaches = weights.shape
    slots = 4
    targets = dest_device.reshape(devices, sources)
    my_targets = lax.dynamic_index_in_dim(targets, my_index, 0, keepdims=False)
    outgoing = map_sources(cell_order.reshape(sources, cells), runoff, my_targets, weights, devices, slots)
    arrived = lax.all_to_all(outgoing.reshape(devices, slots * steps, reaches), ("lat", "lon"),
                             split_axis=0, concat_axis=0, tiled=True)
    arrived = arrived.reshape(devices * slots * steps, reaches)

    vmem = pl.BlockSpec(memory_space=pltpu.VMEM)
    smem = pl.BlockSpec(memory_space=pltpu.SMEM)
    params = pltpu.CompilerParams(vmem_limit_bytes=56 * 1024 * 1024)
    blocks = initial_flow.shape[2]
    plane = (reaches, blocks)

    def made(*shape, dtype=jnp.float32):
        return jax.ShapeDtypeStruct(shape, dtype)

    spread, rows, heads, terms, note, select = pl.pallas_call(
        functools.partial(prepare_kernel, steps, slots),
        out_shape=[made(reaches * reaches, blocks), made(steps, *plane), made(steps, *plane), made(4, *plane),
                   made(32, blocks), made(slots, blocks, devices, dtype=jnp.bfloat16)],
        in_specs=[vmem] * 8 + [smem],
        out_specs=[vmem] * 6,
        scratch_shapes=[pltpu.VMEM(plane, jnp.float32)] * 3,
        compiler_params=params,
        cost_estimate=pl.CostEstimate(flops=2 * 24 * blocks * reaches * reaches, bytes_accessed=20 << 20, transcendentals=0),
    )(
        block_inverse.reshape(blocks * reaches, reaches),
        musk_k.reshape(blocks, reaches),
        musk_x.reshape(blocks, reaches),
        down_reach.reshape(blocks, reaches),
        initial_flow.reshape(blocks, reaches),
        upstream_link.reshape(1, blocks),
        targets,
        dest_block.reshape(devices, sources),
        my_index.reshape(1).astype(jnp.int32),
    )
    lateral, notes = pl.pallas_call(
        functools.partial(lateral_kernel, steps, slots),
        out_shape=[made(steps, *plane), made(lon_count, 32, blocks)],
        in_specs=[vmem] * 4,
        out_specs=[vmem] * 2,
        compiler_params=params,
    )(arrived, select, rows, note)
    notes = lax.all_to_all(notes, "lon", split_axis=0, concat_axis=0, tiled=True)
    flow = pl.pallas_call(
        functools.partial(local_kernel, steps),
        out_shape=made(*plane),
        in_specs=[pl.BlockSpec(memory_space=pl.ANY), vmem, vmem],
        out_specs=vmem,
        scratch_shapes=[pltpu.VMEM(plane, jnp.float32), pltpu.VMEM((reaches * reaches, blocks), jnp.float32),
                        pltpu.SemaphoreType.DMA((8,))],
        compiler_params=params,
        cost_estimate=pl.CostEstimate(flops=2 * 12 * blocks * reaches * reaches, bytes_accessed=10 << 20, transcendentals=0),
    )(spread, terms, lateral)
    result = pl.pallas_call(
        functools.partial(chain_kernel, steps),
        out_shape=made(blocks, reaches),
        in_specs=[vmem] * 3 + [smem],
        out_specs=vmem,
        scratch_shapes=[pltpu.VMEM((lon_count, 32, blocks), jnp.float32)],
        compiler_params=params,
    )(notes, flow, heads, lon_index.reshape(1).astype(jnp.int32))
    return result.reshape(initial_flow.shape)


def solution(mesh):
    return jax.shard_map(
        body,
        mesh=mesh,
        in_specs=(
            P(None, "lat", "lon"),
            P("lat", "lon", None),
            P("lat", "lon", None, None, None),
            P(),
            P(),
            P("lat", "lon", None, None),
            P("lat", "lon", None, None),
            P("lat", "lon", None, None),
            P("lat", "lon", None, None),
            P("lat", "lon", None, None, None),
            P("lat", "lon", None),
        ),
        out_specs=P("lat", "lon", None, None),
        check_vma=False,
    )
```

time: 646 us -> 101 us (0.16); the launches traced: 637 us -> 99.3 us
  blocking collectives: 272 us -> 0 us
  local copies, waits for them, and re-layouts: 173 us -> 3.93 us
  other arithmetic: 153 us -> 0 us
  Pallas kernels: 0 us -> 66.4 us
  matrix products: 14.9 us -> 0 us
  waiting for transfers between devices: 0.01 us -> 13.3 us
  loops' own time: 7.93 us -> 0 us
    all_gather x14 -> x0, blocking collectives: 272 us -> none  [carried_in(): everything = jax.tree.map(lambda part: lax.all_gather(part, axis), array)]
    gather x2 -> x0, local copies, waits for them, and re-layouts: 121 us -> none  [body(): jnp.take(cell_rows, cell_order.reshape(-1), axis=0)]
    pallas_call x0 -> x5, Pallas kernels: none -> 66.4 us  [the longest x1 27.1 us: body(): pl.pallas_call(functools.partial(prepare_kernel, steps, slots), out_shape...]
    dot_general x12 -> x0, other arithmetic: 50.4 us -> none  [body(): local = jnp.einsum('brs,bs->br', inverse, known, precision=highest)]
    unnamed x24 -> x0, other arithmetic: 40.3 us -> none
    reduce_sum x194 -> x0, other arithmetic: 34 us -> none  [the longest x192 32.6 us: select(): return jnp.sum(jnp.where(chosen, values[None, :], 0.0), axis=1)]
    unnamed x49 -> x7, local copies, waits for them, and re-layouts: 32.4 us -> 3.33 us
    dot_general x16 -> x0, matrix products: 14.9 us -> none  [the longest x1 4.67 us: body(): lax.dot_general(picked, weights, (((1,), (1,)), ((0,), (0,))), preferred_...]
  transfers between devices with their start and end apart: 2 -> 2, of which waited for: 0 -> 1; matrix products, arithmetic and copies ran while one was open for 7% -> 0% of each run, Pallas kernels for 0% -> 36%
where the time goes in v1:
time: 101 us; the launch traced here: 99.3 us
  Pallas kernels  66.4 us (66%)
  starting transfers between devices  15.6 us (15%)
  waiting for transfers between devices  13.3 us (13%)
  local copies, waits for them, and re-layouts  3.93 us (4%)
    pallas_call x1, Pallas kernels, body(): pl.pallas_call(functools.partial(prepare_kernel, steps, slots), out_shape...  27.1 us
    pallas_call x1, Pallas kernels, map_sources(): pl.pallas_call(functools.partial(map_kernel, slots), out_shape=jax.ShapeD...  23.6 us
    all_to_all x1, waiting for transfers between devices, body(): lax.all_to_all(outgoing.reshape(devices, slots * steps, reaches), ('lat',...  13.3 us
    all_to_all x1, starting transfers between devices, body(): lax.all_to_all(outgoing.reshape(devices, slots * steps, reaches), ('lat',...  11.1 us
    pallas_call x1, Pallas kernels, body(): pl.pallas_call(functools.partial(local_kernel, steps), out_shape=made(*pl...  8.82 us
    pallas_call x1, Pallas kernels, body(): pl.pallas_call(functools.partial(lateral_kernel, steps, slots), out_shape...  4.66 us
    all_to_all x1, starting transfers between devices, body(): lax.all_to_all(notes, 'lon', split_axis=0, concat_axis=0, tiled=True)  4.48 us
    unnamed x7, local copies, waits for them, and re-layouts  3.33 us
  transfers between devices with their start and end apart: 2, of which 1 were waited for; matrix products, arithmetic and copies ran while one was open for 0% of the time, Pallas kernels for 36%

profile of v1, /device:TPU:0, one launch (start us, length us, event | category | flops | bytes accessed | tf_op | source)
XLA Modules:
  0.0 99.3 jit_solution(18199911636980377066)
XLA Ops:
  0.0 0.9 copy.12
  0.9 0.0 copy-start.2
  0.9 0.6 constant_dynamic-slice_fusion
  1.5 23.6 %shard_map.109 = f32[6144,128]{1,0:T(8,128)} custom-call(s32[256,128]{1,0:T(8,128)} %bitcast.22, bf16[12,128,256]{2,1,0:T(8,128)(2,1)} %runoff_ref.1, s32[256]{0:T(256)} %bitcast.28, bf16[256,128,128]{2,1,0:T(8,128)(2,1)} %bitcast.18), custom_call_target="tpu_custom_call" | custom-call | tf_op jit(solution)/shard_map/pallas_call | solution.py:150
  25.2 0.0 copy-done.2
  25.2 11.1 %all-to-all-start = ((f32[128,48,128]{2,1,0:T(8,128)}), f32[128,48,128]{2,1,0:T(8,128)S(1)}, u32[]{:S(2)}, u32[]{:S(2)}) async-start(f32[128,48,128]{2,1,0:T(8,128)} %bitcast.17), calls=%async_computation | async-start | bytes 6291456 | tf_op jit(solution)/shard_map/all_to_all | solution.py:355
  36.3 27.1 %shard_map.110 = (f32[16384,128]{1,0:T(8,128)}, f32[12,128,128]{2,1,0:T(8,128)}, f32[12,128,128]{2,1,0:T(8,128)}, f32[4,128,128]{2,1,0:T(8,128)}, f32[32,128]{1,0:T(8,128)}, /*index=5*/bf16[4,128,128]{2,1,0:T(8,128)(2,1)}) custom-call(f32[16384,128]{1,0:T(8,128)} %bitcast.19, f32[128,128]{1,0:T(8,128)} %bitcast.24, f32[128,128]{1,0:T(8,128)} %bitcast.25, ...), custom_call_target="tpu_custom_call" | custom-call | flops 100663296 | bytes 20971520 | tf_op jit(solution)/shard_map/pallas_call | solution.py:368
  63.5 13.3 %all-to-all-done = f32[128,48,128]{2,1,0:T(8,128)S(1)} async-done(((f32[128,48,128]{2,1,0:T(8,128)}), f32[128,48,128]{2,1,0:T(8,128)S(1)}, u32[]{:S(2)}, u32[]{:S(2)}) %all-to-all-start) | async-done | bytes 3145760 | tf_op jit(solution)/shard_map/all_to_all | solution.py:355
  76.8 0.0 copy-start
  76.8 1.7 %copy-done = f32[128,48,128]{2,1,0:T(8,128)} copy-done((f32[128,48,128]{2,1,0:T(8,128)}, f32[128,48,128]{2,1,0:T(8,128)S(1)}, u32[]{:S(2)}) %copy-start) | copy-done | bytes 3145752
  78.6 4.7 %shard_map.111 = (f32[12,128,128]{2,1,0:T(8,128)}, f32[16,32,128]{2,1,0:T(8,128)}) custom-call(f32[6144,128]{1,0:T(8,128)} %bitcast.16, bf16[4,128,128]{2,1,0:T(8,128)(2,1)} %get-tuple-element.13.select_ref, f32[12,128,128]{2,1,0:T(8,128)} %get-tuple-element.14.rows_ref, f32[32,128]{1,0:T(8,128)} %get-tuple-element.15.note_ref), custom_call_target="tpu_custom_call" | custom-call | tf_op jit(solution)/shard_map/pallas_call | solution.py:388
  83.2 4.5 %all-to-all-start.1 = ((f32[16,32,128]{2,1,0:T(8,128)}), f32[16,32,128]{2,1,0:T(8,128)S(1)}, u32[]{:S(2)}, u32[]{:S(2)}) async-start(f32[16,32,128]{2,1,0:T(8,128)} %get-tuple-element.16), calls=%async_computation.1 | async-start | bytes 524288 | tf_op jit(solution)/shard_map/all_to_all | solution.py:395
  87.7 8.8 %shard_map.112.flow_ref = f32[128,128]{1,0:T(8,128)} custom-call(f32[16384,128]{1,0:T(8,128)} %get-tuple-element.17.spread_ref, f32[4,128,128]{2,1,0:T(8,128)} %get-tuple-element.18.terms_ref, f32[12,128,128]{2,1,0:T(8,128)} %get-tuple-element.19.lateral_ref), custom_call_target="tpu_custom_call" | custom-call | flops 50331648 | bytes 10485760 | tf_op jit(solution)/shard_map/pallas_call | solution.py:396
  96.5 0.0 all-to-all-done.1.notes_ref
  96.5 0.0 copy-start.1
  96.5 0.7 copy-done.1
  97.2 2.1 %shard_map.113 = f32[128,128]{1,0:T(8,128)} custom-call(f32[16,32,128]{2,1,0:T(8,128)} %copy-done.1, f32[128,128]{1,0:T(8,128)} %shard_map.112.flow_ref, f32[12,128,128]{2,1,0:T(8,128)} %get-tuple-element.20.heads_ref, s32[1]{0:T(128)} %bitcast.13.lon_ref), custom_call_target="tpu_custom_call" | custom-call | tf_op jit(solution)/shard_map/pallas_call | solution.py:406
Async XLA Ops:
  0.9 24.3 %copy-start.2 = (s32[8,16,256,1]{2,1,3,0:T(8,128)}, s32[8,16,256,1]{2,1,3,0:T(8,128)S(1)}, u32[]{:S(2)}) copy-start(s32[8,16,256,1]{2,1,3,0:T(8,128)S(1)} %copy.12) | copy-start | bytes 393220
  25.2 51.6 %all-to-all-start = ((f32[128,48,128]{2,1,0:T(8,128)}), f32[128,48,128]{2,1,0:T(8,128)S(1)}, u32[]{:S(2)}, u32[]{:S(2)}) async-start(f32[128,48,128]{2,1,0:T(8,128)} %bitcast.17), calls=%async_computation | async-start | bytes 6291456 | tf_op jit(solution)/shard_map/all_to_all | solution.py:355
  76.8 1.7 %copy-start = (f32[128,48,128]{2,1,0:T(8,128)}, f32[128,48,128]{2,1,0:T(8,128)S(1)}, u32[]{:S(2)}) copy-start(f32[128,48,128]{2,1,0:T(8,128)S(1)} %all-to-all-done) | copy-start | bytes 9437188
  83.2 13.3 %all-to-all-start.1 = ((f32[16,32,128]{2,1,0:T(8,128)}), f32[16,32,128]{2,1,0:T(8,128)S(1)}, u32[]{:S(2)}, u32[]{:S(2)}) async-start(f32[16,32,128]{2,1,0:T(8,128)} %get-tuple-element.16), calls=%async_computation.1 | async-start | bytes 524288 | tf_op jit(solution)/shard_map/all_to_all | solution.py:395
  96.5 0.7 copy-start.1

commit v2 on v1

--- a/solution.py
+++ b/solution.py
@@ -10,19 +10,31 @@
 
 VREGS = 32
 CHUNKS = 4
+TOGETHER = 6
 
 def gathered(x, index, axis):
     return jnp.take_along_axis(x, index, axis=axis, mode="promise_in_bounds")
 
-def map_kernel(slots, order_ref, runoff_ref, target_ref, weights_ref, out_ref,
-               pick_ref, held_ref, marks_ref, subs_ref, lanes_ref, counts_ref, sems):
+def map_kernel(slots, far_order_ref, grid_ref, target_ref, weights_ref, out_ref,
+               order_ref, runoff_ref, pick_ref, held_ref, marks_ref, subs_ref, lanes_ref, counts_ref, sems):
     sources = weights_ref.shape[0]
     part = sources // CHUNKS
     def fetch(i):
         rows = pl.ds(i * part, part)
         return pltpu.make_async_copy(weights_ref.at[rows], held_ref.at[rows], sems.at[i])
+    order_copy = pltpu.make_async_copy(far_order_ref, order_ref, sems.at[CHUNKS + 1])
+    order_copy.start()
+    grid_copy = pltpu.make_async_copy(grid_ref, runoff_ref, sems.at[CHUNKS])
+    grid_copy.start()
     for i in range(CHUNKS):
         fetch(i).start()
+
+    out_ref[...] = jnp.zeros_like(out_ref)
+    def clear(d, carry):
+        counts_ref[d] = 0
+        return carry
+    lax.fori_loop(0, counts_ref.shape[0], clear, 0)
+    order_copy.wait()
 
     lane = lax.broadcasted_iota(jnp.int32, (8, 128), 1)
     sub = lax.broadcasted_iota(jnp.int32, (8, 128), 0)
@@ -94,40 +106,39 @@
         undo.append((q, pairs))
 
     planes = runoff_ref.shape[0] // 2
-
-    def plane(p, carry):
-        low = (runoff_ref[p].astype(jnp.float32) * 4096.0).astype(jnp.int32)
-        high = (runoff_ref[p + planes].astype(jnp.float32) * 4096.0).astype(jnp.int32)
-        both = low | (high << 16)
-        x = []
-        for h in range(2):
-            for r in range(16):
-                x.append(both[8 * r:8 * r + 8, 128 * h:128 * h + 128])
+    grid_copy.wait()
+
+    def several(g, carry):
+        first = g * TOGETHER
+        xs = []
+        for n in range(TOGETHER):
+            p = first + n
+            low = (runoff_ref[p].astype(jnp.float32) * 4096.0).astype(jnp.int32)
+            high = (runoff_ref[p + planes].astype(jnp.float32) * 4096.0).astype(jnp.int32)
+            both = low | (high << 16)
+            xs.append([both[8 * r:8 * r + 8, 128 * h:128 * h + 128] for h in range(2) for r in range(16)])
         for q, pairs in reversed(undo):
-            for at, v, w in reversed(pairs):
-                mark = marks_ref[at] != 0
-                x[v], x[w] = jnp.where(mark, x[w], x[v]), jnp.where(mark, x[v], x[w])
-            if q >= 6:
+            for x in xs:
+                for at, v, w in reversed(pairs):
+                    mark = marks_ref[at] != 0
+                    x[v], x[w] = jnp.where(mark, x[w], x[v]), jnp.where(mark, x[v], x[w])
                 for v in range(VREGS):
-                    x[v] = gathered(x[v], subs_ref[(q - 6) * VREGS + v], 0)
-            if q >= 9:
-                for v in range(VREGS):
-                    x[v] = gathered(x[v], lanes_ref[(q - 9) * VREGS + v], 1)
+                    if q >= 6:
+                        x[v] = gathered(x[v], subs_ref[(q - 6) * VREGS + v], 0)
+                    if q >= 9:
+                        x[v] = gathered(x[v], lanes_ref[(q - 9) * VREGS + v], 1)
         scale = 1.0 / 4096.0
-        for v in range(VREGS):
-            pick_ref[pl.ds(128 * v + p, 8, stride=16), :] = (x[v] & 0xFFFF).astype(jnp.float32) * scale
-            pick_ref[pl.ds(128 * v + p + planes, 8, stride=16), :] = (x[v] >> 16).astype(jnp.float32) * scale
+        for n, x in enumerate(xs):
+            for v in range(VREGS):
+                p = 128 * v + first + n
+                pick_ref[pl.ds(p, 8, stride=16), :] = (x[v] & 0xFFFF).astype(jnp.float32) * scale
+                pick_ref[pl.ds(p + planes, 8, stride=16), :] = (x[v] >> 16).astype(jnp.float32) * scale
         return carry
 
-    lax.fori_loop(0, planes, plane, 0)
-
-    out_ref[...] = jnp.zeros_like(out_ref)
-    def clear(d, carry):
-        counts_ref[d] = 0
-        return carry
-    lax.fori_loop(0, counts_ref.shape[0], clear, 0)
+    lax.fori_loop(0, planes // TOGETHER, several, 0)
+
     steps = 2 * planes
-    unroll = 8
+    unroll = 64
     for i in range(CHUNKS):
         fetch(i).wait()
         def group(g, carry):
@@ -147,22 +158,26 @@
     steps = runoff.shape[0]
     sources, cells, reaches = weights.shape
     vmem = pl.BlockSpec(memory_space=pltpu.VMEM)
+    far = pl.BlockSpec(memory_space=pltpu.HBM)
     return pl.pallas_call(
         functools.partial(map_kernel, slots),
         out_shape=jax.ShapeDtypeStruct((devices * slots * steps, reaches), jnp.float32),
-        in_specs=[vmem, vmem, pl.BlockSpec(memory_space=pltpu.SMEM), pl.BlockSpec(memory_space=pl.ANY)],
+        in_specs=[far, far, pl.BlockSpec(memory_space=pltpu.SMEM), far],
         out_specs=vmem,
         scratch_shapes=[
+            pltpu.VMEM(order.shape, order.dtype),
+            pltpu.VMEM(runoff.shape, runoff.dtype),
             pltpu.VMEM((sources * 16, cells), jnp.float32),
             pltpu.VMEM(weights.shape, weights.dtype),
             pltpu.VMEM((1040, 8, 128), jnp.int32),
             pltpu.VMEM((10 * VREGS, 8, 128), jnp.int32),
             pltpu.VMEM((7 * VREGS, 8, 128), jnp.int32),
             pltpu.SMEM((devices,), jnp.int32),
-            pltpu.SemaphoreType.DMA((CHUNKS,)),
+            pltpu.SemaphoreType.DMA((CHUNKS + 2,)),
         ],
-        compiler_params=pltpu.CompilerParams(vmem_limit_bytes=56 * 1024 * 1024),
-    )(order, runoff, target, weights)
+        compiler_params=pltpu.CompilerParams(vmem_limit_bytes=52 << 20),
+    )(pltpu.with_memory_space_constraint(order, pltpu.HBM), pltpu.with_memory_space_constraint(runoff, pltpu.HBM), target,
+      pltpu.with_memory_space_constraint(weights, pltpu.HBM))
 
 
 def coefficients(travel, weighting):
@@ -179,8 +194,8 @@
 
 
 def prepare_kernel(steps, slots, inverse_ref, travel_ref, weighting_ref, drains_ref, flow_ref, links_ref,
-                   targets_ref, blocks_ref, me_ref, spread_ref, rows_ref, heads_ref, terms_ref, note_ref,
-                   select_ref, left_ref, scaled_ref, product_ref):
+                   targets_ref, blocks_ref, me_ref, spread_ref, rows_ref, heads_ref, terms_ref, far_note_ref,
+                   note_ref, left_ref, scaled_ref, product_ref, sem):
     first, second, third = coefficients(travel_ref[...], weighting_ref[...])
     drains = drains_ref[...]
     nearest = jnp.minimum(drains, SIZE - 1)
@@ -203,12 +218,11 @@
     order = lax.broadcasted_iota(jnp.int32, (sources, sources), 0)
     later = (order <= lax.broadcasted_iota(jnp.int32, (sources, sources), 1)).astype(jnp.bfloat16)
     place = jnp.dot(hits.astype(jnp.bfloat16), later, preferred_element_type=jnp.float32)
-    column = lax.broadcasted_iota(jnp.int32, (SIZE, SIZE), 1).astype(jnp.float32)
     numbers = blocks_ref[...].astype(jnp.float32) + 1.0
     for k in range(slots):
         here = hits & (place == k + 1.0)
         named = jnp.sum(jnp.where(here, numbers, 0.0), axis=1, keepdims=True) - 1.0
-        select_ref[k] = (named == column).astype(jnp.float32).T.astype(jnp.bfloat16)
+        note_ref[32 + k:33 + k, :] = jnp.broadcast_to(named, (SIZE, SIZE)).T[0:1, :]
 
     def turned(g, carry):
         for u in range(4):
@@ -249,10 +263,21 @@
         return carry
 
     lax.fori_loop(0, steps, power, 0)
-
-
-def lateral_kernel(steps, slots, arrived_ref, select_ref, rows_ref, note_ref, lateral_ref, notes_ref):
+    store = pltpu.make_async_copy(note_ref, far_note_ref, sem)
+    store.start()
+    store.wait()
+
+
+def lateral_kernel(steps, slots, arrived_ref, far_note_ref, far_rows_ref, far_lateral_ref, far_notes_ref,
+                   note_ref, rows_ref, lateral_ref, notes_ref, sems):
+    opening = pltpu.make_async_copy(far_note_ref, note_ref, sems.at[2])
+    opening.start()
+    fetch = pltpu.make_async_copy(far_rows_ref, rows_ref, sems.at[0])
+    fetch.start()
     sources = arrived_ref.shape[0] // (slots * steps)
+    opening.wait()
+    block = lax.broadcasted_iota(jnp.int32, (SIZE, sources), 0).astype(jnp.float32)
+    select = [(note_ref[32 + k:33 + k, :] == block).astype(jnp.bfloat16) for k in range(slots)]
     for t in range(steps):
         total = None
         for k in range(slots):
@@ -260,9 +285,12 @@
             high = piece.astype(jnp.bfloat16)
             low = (piece - high.astype(jnp.float32)).astype(jnp.bfloat16)
             for part in (high, low):
-                term = jnp.dot(select_ref[k], part, preferred_element_type=jnp.float32)
+                term = jnp.dot(select[k], part, preferred_element_type=jnp.float32)
                 total = term if total is None else total + term
         lateral_ref[t] = total.T
+    store = pltpu.make_async_copy(lateral_ref, far_lateral_ref, sems.at[1])
+    store.start()
+    fetch.wait()
     sums = [jnp.zeros((8, SIZE), jnp.float32) for _ in range(steps)]
     for i in range(TILES):
         tile = slice(8 * i, 8 * i + 8)
@@ -271,33 +299,40 @@
         for t in range(steps):
             for j in range(t + 1):
                 sums[t] = sums[t] + weight[t - j] * given[j]
-    note = note_ref[...]
+    note = note_ref[0:32, :]
     series = [jnp.sum(part, axis=0, keepdims=True) for part in sums]
     whole = jnp.concatenate(
         [note[0:1]] + [note[1 + t:2 + t] + series[t] for t in range(steps)] + [note[1 + steps:]], axis=0)
     for d in range(notes_ref.shape[0]):
         notes_ref[d] = whole
-
-
-def local_kernel(steps, spread_ref, terms_ref, lateral_ref, flow_ref, scaled_ref, held_ref, sems):
-    def fetch(i):
-        rows = pl.ds(i * 2048, 2048)
-        return pltpu.make_async_copy(spread_ref.at[rows], held_ref.at[rows], sems.at[i])
-
-    for i in range(8):
-        fetch(i).start()
+    send = pltpu.make_async_copy(notes_ref, far_notes_ref, sems.at[3])
+    send.start()
+    send.wait()
+    store.wait()
+
+
+def local_kernel(steps, terms_ref, far_spread_ref, far_lateral_ref, flow_ref, spread_ref, lateral_ref, scaled_ref, sems):
+    def fetch(j):
+        where = (pl.ds(8 * j, 8), pl.ds(8 * j, SIZE - 8 * j))
+        return pltpu.make_async_copy(far_spread_ref.at[where], spread_ref.at[where], sems.at[j])
+
+    given = pltpu.make_async_copy(far_lateral_ref, lateral_ref, sems.at[TILES])
+    given.start()
+    for j in range(TILES):
+        fetch(j).start()
     flow_ref[...] = terms_ref[3]
-
-    def step(t, wait):
+    given.wait()
+
+    def step(t, first):
         flow = flow_ref[...]
         scaled_ref[...] = terms_ref[0] * flow + terms_ref[2] * lateral_ref[t]
         sums = [jnp.zeros((8, SIZE), jnp.float32) for _ in range(TILES)]
         for s in range(SIZE):
-            if wait and s % 16 == 0:
-                fetch(s // 16).wait()
+            if first and s % 8 == 0:
+                fetch(s // 8).wait()
             factor = scaled_ref[s:s + 1, :]
             for i in range(s // 8, TILES):
-                sums[i] = sums[i] + held_ref[s * SIZE + 8 * i:s * SIZE + 8 * i + 8, :] * factor
+                sums[i] = sums[i] + spread_ref[s, 8 * i:8 * i + 8, :] * factor
         flow_ref[...] = jnp.concatenate(sums, axis=0) - terms_ref[1] * flow
 
     step(0, True)
@@ -309,7 +344,9 @@
     lax.fori_loop(1, steps, rest, 0)
 
 
-def chain_kernel(steps, notes_ref, flow_ref, heads_ref, lon_ref, out_ref, pad_ref):
+def chain_kernel(steps, notes_ref, flow_ref, far_heads_ref, lon_ref, out_ref, pad_ref, heads_ref, sem):
+    fetch = pltpu.make_async_copy(far_heads_ref, heads_ref, sem)
+    fetch.start()
     count = notes_ref.shape[0]
     me = lon_ref[0]
     row = lax.broadcasted_iota(jnp.int32, (16, SIZE), 0)
@@ -333,6 +370,7 @@
 
     series = lax.fori_loop(1, me, hop, notes_ref[0, 0:16, :])
     entering = jnp.where(me > 0, inlet(me, series), 0.0)
+    fetch.wait()
     flow = flow_ref[...]
     for t in range(1, steps + 1):
         flow = flow + heads_ref[steps - t] * entering[t:t + 1, :]
@@ -350,7 +388,8 @@
     sources, cells, reaches = weights.shape
     slots = 4
     targets = dest_device.reshape(devices, sources)
-    my_targets = lax.dynamic_index_in_dim(targets, my_index, 0, keepdims=False)
+    my_targets = lax.dynamic_slice(dest_device, (lax.axis_index("lat"), lon_index, 0, 0), (1, 1, sources, 1))
+    my_targets = my_targets.reshape(sources)
     outgoing = map_sources(cell_order.reshape(sources, cells), runoff, my_targets, weights, devices, slots)
     arrived = lax.all_to_all(outgoing.reshape(devices, slots * steps, reaches), ("lat", "lon"),
                              split_axis=0, concat_axis=0, tiled=True)
@@ -358,21 +397,32 @@
 
     vmem = pl.BlockSpec(memory_space=pltpu.VMEM)
     smem = pl.BlockSpec(memory_space=pltpu.SMEM)
-    params = pltpu.CompilerParams(vmem_limit_bytes=56 * 1024 * 1024)
+
+    def params(mib):
+        return pltpu.CompilerParams(vmem_limit_bytes=mib << 20)
+
+    def near(x):
+        return pltpu.with_memory_space_constraint(x, pltpu.VMEM)
+
+    def away(x):
+        return pltpu.with_memory_space_constraint(x, pltpu.HBM)
+
+    far = pl.BlockSpec(memory_space=pltpu.HBM)
     blocks = initial_flow.shape[2]
     plane = (reaches, blocks)
-
-    def made(*shape, dtype=jnp.float32):
-        return jax.ShapeDtypeStruct(shape, dtype)
-
-    spread, rows, heads, terms, note, select = pl.pallas_call(
+    moves = pltpu.SemaphoreType.DMA
+
+    def made(*shape):
+        return jax.ShapeDtypeStruct(shape, jnp.float32)
+
+    spread, rows, heads, terms, note = pl.pallas_call(
         functools.partial(prepare_kernel, steps, slots),
         out_shape=[made(reaches * reaches, blocks), made(steps, *plane), made(steps, *plane), made(4, *plane),
-                   made(32, blocks), made(slots, blocks, devices, dtype=jnp.bfloat16)],
+                   pltpu.HBM((40, blocks), jnp.float32)],
         in_specs=[vmem] * 8 + [smem],
-        out_specs=[vmem] * 6,
-        scratch_shapes=[pltpu.VMEM(plane, jnp.float32)] * 3,
-        compiler_params=params,
+        out_specs=[vmem] * 4 + [far],
+        scratch_shapes=[pltpu.VMEM((40, blocks), jnp.float32)] + [pltpu.VMEM(plane, jnp.float32)] * 3 + [moves],
+        compiler_params=params(52),
         cost_estimate=pl.CostEstimate(flops=2 * 24 * blocks * reaches * reaches, bytes_accessed=20 << 20, transcendentals=0),
     )(
         block_inverse.reshape(blocks * reaches, reaches),
@@ -387,30 +437,32 @@
     )
     lateral, notes = pl.pallas_call(
         functools.partial(lateral_kernel, steps, slots),
-        out_shape=[made(steps, *plane), made(lon_count, 32, blocks)],
-        in_specs=[vmem] * 4,
-        out_specs=[vmem] * 2,
-        compiler_params=params,
-    )(arrived, select, rows, note)
+        out_shape=[pltpu.HBM((steps, *plane), jnp.float32), pltpu.HBM((lon_count, 32, blocks), jnp.float32)],
+        in_specs=[vmem, far, far],
+        out_specs=[far, far],
+        scratch_shapes=[pltpu.VMEM((40, blocks), jnp.float32)] + [pltpu.VMEM((steps, *plane), jnp.float32)] * 2
+        + [pltpu.VMEM((lon_count, 32, blocks), jnp.float32), moves((4,))],
+        compiler_params=params(10),
+    )(near(arrived), away(note), away(rows))
     notes = lax.all_to_all(notes, "lon", split_axis=0, concat_axis=0, tiled=True)
     flow = pl.pallas_call(
         functools.partial(local_kernel, steps),
         out_shape=made(*plane),
-        in_specs=[pl.BlockSpec(memory_space=pl.ANY), vmem, vmem],
+        in_specs=[vmem, far, far],
         out_specs=vmem,
-        scratch_shapes=[pltpu.VMEM(plane, jnp.float32), pltpu.VMEM((reaches * reaches, blocks), jnp.float32),
-                        pltpu.SemaphoreType.DMA((8,))],
-        compiler_params=params,
-        cost_estimate=pl.CostEstimate(flops=2 * 12 * blocks * reaches * reaches, bytes_accessed=10 << 20, transcendentals=0),
-    )(spread, terms, lateral)
+        scratch_shapes=[pltpu.VMEM((reaches, *plane), jnp.float32), pltpu.VMEM((steps, *plane), jnp.float32),
+                        pltpu.VMEM(plane, jnp.float32), moves((TILES + 1,))],
+        compiler_params=params(52),
+        cost_estimate=pl.CostEstimate(flops=2 * 12 * blocks * reaches * reaches, bytes_accessed=8 << 20, transcendentals=0),
+    )(terms, away(spread.reshape(reaches, *plane)), away(lateral))
     result = pl.pallas_call(
         functools.partial(chain_kernel, steps),
         out_shape=made(blocks, reaches),
-        in_specs=[vmem] * 3 + [smem],
+        in_specs=[vmem, vmem, far, smem],
         out_specs=vmem,
-        scratch_shapes=[pltpu.VMEM((lon_count, 32, blocks), jnp.float32)],
-        compiler_params=params,
-    )(notes, flow, heads, lon_index.reshape(1).astype(jnp.int32))
+        scratch_shapes=[pltpu.VMEM((lon_count, 32, blocks), jnp.float32), pltpu.VMEM((steps, *plane), jnp.float32), moves],
+        compiler_params=params(10),
+    )(near(notes), flow, away(heads), lon_index.reshape(1).astype(jnp.int32))
     return result.reshape(initial_flow.shape)
 
 

time: 101 us -> 87 us (0.86); the launches traced: 99.3 us -> 86.4 us
  Pallas kernels: 66.4 us -> 53.9 us
  waiting for transfers between devices: 13.3 us -> 10.8 us
  local copies, waits for them, and re-layouts: 3.93 us -> 5.86 us
    pallas_call x1, Pallas kernels: 23.6 us -> 15.9 us  [map_sources(): pl.pallas_call(functools.partial(map_kernel, slots), out_shape=jax.ShapeD...]
    all_to_all x1, waiting for transfers between devices: 13.3 us -> 8.41 us  [body(): lax.all_to_all(outgoing.reshape(devices, slots * steps, reaches), ('lat',...]
    pallas_call x1, Pallas kernels: 8.82 us -> 6.12 us  [body(): pl.pallas_call(functools.partial(local_kernel, steps), out_shape=made(*pl...]
    all_to_all x1, waiting for transfers between devices: 0.01 us -> 2.39 us  [body(): lax.all_to_all(notes, 'lon', split_axis=0, concat_axis=0, tiled=True)]
    unnamed x7 -> x17, local copies, waits for them, and re-layouts: 3.33 us -> 5.18 us
    pallas_call x1, Pallas kernels: 4.66 us -> 3.14 us  [body(): pl.pallas_call(functools.partial(lateral_kernel, steps, slots), out_shape...]
  transfers between devices with their start and end apart: 2 -> 2, of which waited for: 1 -> 2; matrix products, arithmetic and copies ran while one was open for 0% -> 0% of each run, Pallas kernels for 36% -> 38%
where the time goes in v2:
time: 87 us; the launch traced here: 86.4 us
  Pallas kernels  53.9 us (62%)
  starting transfers between devices  15.6 us (18%)
  waiting for transfers between devices  10.8 us (12%)
  local copies, waits for them, and re-layouts  5.86 us (7%)
    pallas_call x1, Pallas kernels, body(): pl.pallas_call(functools.partial(prepare_kernel, steps, slots), out_shape...  26.8 us
    pallas_call x1, Pallas kernels, map_sources(): pl.pallas_call(functools.partial(map_kernel, slots), out_shape=jax.ShapeD...  15.9 us
    all_to_all x1, starting transfers between devices, body(): lax.all_to_all(outgoing.reshape(devices, slots * steps, reaches), ('lat',...  11.1 us
    all_to_all x1, waiting for transfers between devices, body(): lax.all_to_all(outgoing.reshape(devices, slots * steps, reaches), ('lat',...  8.41 us
    pallas_call x1, Pallas kernels, body(): pl.pallas_call(functools.partial(local_kernel, steps), out_shape=made(*pl...  6.12 us
    unnamed x17, local copies, waits for them, and re-layouts  5.18 us
    all_to_all x1, starting transfers between devices, body(): lax.all_to_all(notes, 'lon', split_axis=0, concat_axis=0, tiled=True)  4.49 us
    pallas_call x1, Pallas kernels, body(): pl.pallas_call(functools.partial(lateral_kernel, steps, slots), out_shape...  3.14 us
  transfers between devices with their start and end apart: 2, of which 2 were waited for; matrix products, arithmetic and copies ran while one was open for 0% of the time, Pallas kernels for 38%

profile of v2, /device:TPU:0, one launch (start us, length us, event | category | flops | bytes accessed | tf_op | source)
XLA Modules:
  0.0 86.4 jit_solution(325096379397549247)
XLA Ops:
  0.0 0.7 constant_dynamic-slice_fusion
  0.7 0.0 copy-start.7
  0.7 0.0 copy-start.6
  0.7 15.9 %shard_map.109 = f32[6144,128]{1,0:T(8,128)} custom-call(s32[256,128]{1,0:T(8,128)} %bitcast.30, bf16[12,128,256]{2,1,0:T(8,128)(2,1)} %grid_ref.1, s32[256]{0:T(256)S(1)} %bitcast.24, bf16[256,128,128]{2,1,0:T(8,128)(2,1)} %bitcast.27), custom_call_target="tpu_custom_call" | custom-call | tf_op jit(solution)/shard_map/pallas_call | solution.py:162
  16.6 11.1 %all-to-all-start = ((f32[128,48,128]{2,1,0:T(8,128)}), f32[128,48,128]{2,1,0:T(8,128)S(1)}, u32[]{:S(2)}, u32[]{:S(2)}) async-start(f32[128,48,128]{2,1,0:T(8,128)} %bitcast.26), calls=%async_computation | async-start | bytes 6291456 | tf_op jit(solution)/shard_map/all_to_all | solution.py:394
  27.7 0.0 copy-done.7
  27.8 0.0 copy-done.6
  27.8 0.0 copy-start.1
  27.8 0.9 %copy-done.1 = s32[8,16,256]{2,1,0:T(8,128)S(1)} copy-done((s32[8,16,256]{2,1,0:T(8,128)S(1)}, s32[8,16,256]{2,1,0:T(8,128)}, u32[]{:S(2)}) %copy-start.1) | copy-done | bytes 131096
  28.7 0.0 copy-start.2
  28.7 0.8 copy-done.2
  29.5 0.0 copy-start.3
  29.5 0.8 copy-done.3
  30.4 0.0 copy-start.4
  30.4 0.8 copy-done.4
  31.2 0.0 copy-start.5
  31.2 0.8 copy-done.5
  32.1 26.8 %shard_map.110 = (f32[16384,128]{1,0:T(8,128)}, f32[12,128,128]{2,1,0:T(8,128)S(1)}, f32[12,128,128]{2,1,0:T(8,128)}, f32[4,128,128]{2,1,0:T(8,128)S(1)}, f32[40,128]{1,0:T(8,128)}) custom-call(f32[16384,128]{1,0:T(8,128)} %bitcast.28, f32[128,128]{1,0:T(8,128)S(1)} %bitcast.20, f32[128,128]{1,0:T(8,128)S(1)} %bitcast.21, s32[128,128]{1,0:T(8,128)S(1)} %bitcast.22, ...), custom_call_target="tpu_custom_call" | custom-call | flops 100663296 | bytes 20971520 | tf_op jit(solution)/shard_map/pallas_call | solution.py:418
  58.9 0.0 copy-start
  58.9 0.9 %copy-done = f32[12,128,128]{2,1,0:T(8,128)} copy-done((f32[12,128,128]{2,1,0:T(8,128)}, f32[12,128,128]{2,1,0:T(8,128)S(1)}, u32[]{:S(2)}) %copy-start) | copy-done | bytes 786456
  59.8 8.4 %all-to-all-done = f32[128,48,128]{2,1,0:T(8,128)S(1)} async-done(((f32[128,48,128]{2,1,0:T(8,128)}), f32[128,48,128]{2,1,0:T(8,128)S(1)}, u32[]{:S(2)}, u32[]{:S(2)}) %all-to-all-start) | async-done | bytes 3145760 | tf_op jit(solution)/shard_map/all_to_all | solution.py:394
  68.2 3.1 %shard_map.111 = (f32[12,128,128]{2,1,0:T(8,128)}, f32[16,32,128]{2,1,0:T(8,128)}) custom-call(f32[6144,128]{1,0:T(8,128)S(1)} %bitcast.17, f32[40,128]{1,0:T(8,128)} %get-tuple-element.12.far_note_ref, f32[12,128,128]{2,1,0:T(8,128)} %copy-done), custom_call_target="tpu_custom_call" | custom-call | tf_op jit(solution)/shard_map/pallas_call | solution.py:438
  71.4 4.5 %all-to-all-start.1 = ((f32[16,32,128]{2,1,0:T(8,128)}), f32[16,32,128]{2,1,0:T(8,128)S(1)}, u32[]{:S(2)}, u32[]{:S(2)}) async-start(f32[16,32,128]{2,1,0:T(8,128)} %get-tuple-element.14), calls=%async_computation.1 | async-start | bytes 524288 | tf_op jit(solution)/shard_map/all_to_all | solution.py:447
  75.9 6.1 %shard_map.112.flow_ref = f32[128,128]{1,0:T(8,128)S(1)} custom-call(f32[4,128,128]{2,1,0:T(8,128)S(1)} %get-tuple-element.15.terms_ref, f32[128,128,128]{2,1,0:T(8,128)} %bitcast.29, f32[12,128,128]{2,1,0:T(8,128)} %get-tuple-element.17.far_lateral_ref), custom_call_target="tpu_custom_call" | custom-call | flops 50331648 | bytes 8388608 | tf_op jit(solution)/shard_map/pallas_call | solution.py:448
  82.0 2.4 %all-to-all-done.1.notes_ref = f32[16,32,128]{2,1,0:T(8,128)S(1)} async-done(((f32[16,32,128]{2,1,0:T(8,128)}), f32[16,32,128]{2,1,0:T(8,128)S(1)}, u32[]{:S(2)}, u32[]{:S(2)}) %all-to-all-start.1) | async-done | bytes 262176 | tf_op jit(solution)/shard_map/all_to_all | solution.py:447
  84.4 1.9 %shard_map.113 = f32[128,128]{1,0:T(8,128)} custom-call(f32[16,32,128]{2,1,0:T(8,128)S(1)} %all-to-all-done.1.notes_ref, f32[128,128]{1,0:T(8,128)S(1)} %shard_map.112.flow_ref, f32[12,128,128]{2,1,0:T(8,128)} %get-tuple-element.18.far_heads_ref, s32[1]{0:T(128)} %bitcast.14.lon_ref), custom_call_target="tpu_custom_call" | custom-call | tf_op jit(solution)/shard_map/pallas_call | solution.py:458
  (1 shorter events, 0.0 us)
Async XLA Ops:
  0.7 27.1 %copy-start.7 = (s32[8,16,256,1]{2,3,1,0:T(1,128)S(1)}, s32[8,16,256,1]{2,3,1,0:T(1,128)}, u32[]{:S(2)}) copy-start(s32[8,16,256,1]{2,3,1,0:T(1,128)} %param.14) | copy-start | bytes 393220
  0.7 27.1 %copy-start.6 = (s32[1,1,128]{2,1,0:T(1,128)S(1)}, s32[1,1,128]{2,1,0:T(1,128)}, u32[]{:S(2)}) copy-start(s32[1,1,128]{2,1,0:T(1,128)} %param.21) | copy-start | bytes 1540
  16.6 51.6 %all-to-all-start = ((f32[128,48,128]{2,1,0:T(8,128)}), f32[128,48,128]{2,1,0:T(8,128)S(1)}, u32[]{:S(2)}, u32[]{:S(2)}) async-start(f32[128,48,128]{2,1,0:T(8,128)} %bitcast.26), calls=%async_computation | async-start | bytes 6291456 | tf_op jit(solution)/shard_map/all_to_all | solution.py:394
  27.8 0.9 %copy-start.1 = (s32[8,16,256]{2,1,0:T(8,128)S(1)}, s32[8,16,256]{2,1,0:T(8,128)}, u32[]{:S(2)}) copy-start(s32[8,16,256]{2,1,0:T(8,128)} %param.15) | copy-start | bytes 393220
  28.7 0.8 copy-start.2
  29.5 0.8 copy-start.3
  30.4 0.8 copy-start.4
  31.2 0.8 copy-start.5
  58.9 0.9 %copy-start = (f32[12,128,128]{2,1,0:T(8,128)}, f32[12,128,128]{2,1,0:T(8,128)S(1)}, u32[]{:S(2)}) copy-start(f32[12,128,128]{2,1,0:T(8,128)S(1)} %get-tuple-element.13.far_rows_ref) | copy-start | bytes 2359300
  71.4 13.0 %all-to-all-start.1 = ((f32[16,32,128]{2,1,0:T(8,128)}), f32[16,32,128]{2,1,0:T(8,128)S(1)}, u32[]{:S(2)}, u32[]{:S(2)}) async-start(f32[16,32,128]{2,1,0:T(8,128)} %get-tuple-element.14), calls=%async_computation.1 | async-start | bytes 524288 | tf_op jit(solution)/shard_map/all_to_all | solution.py:447

commit v3 on v2

--- a/solution.py
+++ b/solution.py
@@ -15,8 +15,8 @@
 def gathered(x, index, axis):
     return jnp.take_along_axis(x, index, axis=axis, mode="promise_in_bounds")
 
-def map_kernel(slots, far_order_ref, grid_ref, target_ref, weights_ref, out_ref,
-               order_ref, runoff_ref, pick_ref, held_ref, marks_ref, subs_ref, lanes_ref, counts_ref, sems):
+def map_kernel(slots, far_order_ref, grid_ref, owners_ref, me_ref, weights_ref, out_ref,
+               target_ref, order_ref, runoff_ref, pick_ref, held_ref, marks_ref, subs_ref, lanes_ref, counts_ref, sems):
     sources = weights_ref.shape[0]
     part = sources // CHUNKS
     def fetch(i):
@@ -24,6 +24,13 @@
         return pltpu.make_async_copy(weights_ref.at[rows], held_ref.at[rows], sems.at[i])
     order_copy = pltpu.make_async_copy(far_order_ref, order_ref, sems.at[CHUNKS + 1])
     order_copy.start()
+    per_device = weights_ref.shape[0] // 128
+    first_row = me_ref[0] * per_device
+    aligned = (first_row >> 3) << 3
+    within = first_row - aligned
+    target_copy = pltpu.make_async_copy(
+        owners_ref.at[pl.ds(pl.multiple_of(aligned, 8), 8)], target_ref, sems.at[CHUNKS + 2])
+    target_copy.start()
     grid_copy = pltpu.make_async_copy(grid_ref, runoff_ref, sems.at[CHUNKS])
     grid_copy.start()
     for i in range(CHUNKS):
@@ -86,12 +93,14 @@
                     marks[v].append((new != keys[v], partner))
                     keys[v] = new
             row = (q - 9) if axis == 1 else (q - 6)
+            index = [place] * VREGS
+            for n in reversed(range(len(bits))):
+                for v in range(VREGS):
+                    mark, partner = marks[v][n]
+                    other = partner if index[v] is place else gathered(index[v], partner, axis)
+                    index[v] = jnp.where(mark, other, index[v])
             for v in range(VREGS):
-                index = place
-                for mark, partner in reversed(marks[v]):
-                    other = partner if index is place else gathered(index, partner, axis)
-                    index = jnp.where(mark, other, index)
-                ref[row * VREGS + v] = index
+                ref[row * VREGS + v] = index[v]
         pairs = []
         for k in range(min(q - 1, 4), -1, -1):
             for v in range(VREGS):
@@ -118,15 +127,22 @@
             both = low | (high << 16)
             xs.append([both[8 * r:8 * r + 8, 128 * h:128 * h + 128] for h in range(2) for r in range(16)])
         for q, pairs in reversed(undo):
-            for x in xs:
+            for base in range(0, TOGETHER, 2):
+                some = xs[base:base + 2]
                 for at, v, w in reversed(pairs):
                     mark = marks_ref[at] != 0
-                    x[v], x[w] = jnp.where(mark, x[w], x[v]), jnp.where(mark, x[v], x[w])
+                    for x in some:
+                        x[v], x[w] = jnp.where(mark, x[w], x[v]), jnp.where(mark, x[v], x[w])
                 for v in range(VREGS):
                     if q >= 6:
-                        x[v] = gathered(x[v], subs_ref[(q - 6) * VREGS + v], 0)
-                    if q >= 9:
-                        x[v] = gathered(x[v], lanes_ref[(q - 9) * VREGS + v], 1)
+                        index = subs_ref[(q - 6) * VREGS + v]
+                        for x in some:
+                            x[v] = gathered(x[v], index, 0)
+            if q >= 9:
+                for v in range(VREGS):
+                    index = lanes_ref[(q - 9) * VREGS + v]
+                    for x in xs:
+                        x[v] = gathered(x[v], index, 1)
         scale = 1.0 / 4096.0
         for n, x in enumerate(xs):
             for v in range(VREGS):
@@ -137,24 +153,32 @@
 
     lax.fori_loop(0, planes // TOGETHER, several, 0)
 
+    target_copy.wait()
     steps = 2 * planes
     unroll = 64
     for i in range(CHUNKS):
         fetch(i).wait()
         def group(g, carry):
-            for u in range(unroll):
+            for u in range(0, unroll, 2):
                 s = i * part + g * unroll + u
-                lhs = pick_ref[pl.ds(pl.multiple_of(s * 16, 16), 16), :].astype(jnp.bfloat16)
-                c = jnp.dot(lhs, held_ref[s], preferred_element_type=jnp.float32)
-                d = target_ref[s]
-                k = counts_ref[d]
-                counts_ref[d] = k + 1
-                out_ref[pl.ds(d * (slots * steps) + k, steps, stride=slots), :] = c[:steps]
+                rows = pick_ref[pl.ds(pl.multiple_of(s * 16, 32), 32), :].astype(jnp.bfloat16)
+                none = jnp.zeros((16, 128), jnp.bfloat16)
+                lhs = jnp.concatenate([jnp.concatenate([rows[:16], none], 1), jnp.concatenate([none, rows[16:]], 1)], 0)
+                both = jnp.dot(lhs, held_ref[pl.ds(s, 2)].reshape(256, 128), preferred_element_type=jnp.float32)
+                for n in range(2):
+                    d = target_ref[within + ((s + n) >> 7), (s + n) & 127]
+                    k = counts_ref[d]
+                    counts_ref[d] = k + 1
+                    out_ref[pl.ds(d * (slots * steps) + k, steps, stride=slots), :] = both[16 * n:16 * n + steps]
             return carry
         lax.fori_loop(0, part // unroll, group, 0)
 
 
-def map_sources(order, runoff, target, weights, devices, slots):
+def away(x):
+    return pltpu.with_memory_space_constraint(x, pltpu.HBM)
+
+
+def map_sources(order, runoff, owners, me, weights, devices, slots):
     steps = runoff.shape[0]
     sources, cells, reaches = weights.shape
     vmem = pl.BlockSpec(memory_space=pltpu.VMEM)
@@ -162,9 +186,10 @@
     return pl.pallas_call(
         functools.partial(map_kernel, slots),
         out_shape=jax.ShapeDtypeStruct((devices * slots * steps, reaches), jnp.float32),
-        in_specs=[far, far, pl.BlockSpec(memory_space=pltpu.SMEM), far],
+        in_specs=[far, far, far, pl.BlockSpec(memory_space=pltpu.SMEM), far],
         out_specs=vmem,
         scratch_shapes=[
+            pltpu.SMEM((8, 128), jnp.int32),
             pltpu.VMEM(order.shape, order.dtype),
             pltpu.VMEM(runoff.shape, runoff.dtype),
             pltpu.VMEM((sources * 16, cells), jnp.float32),
@@ -173,11 +198,10 @@
             pltpu.VMEM((10 * VREGS, 8, 128), jnp.int32),
             pltpu.VMEM((7 * VREGS, 8, 128), jnp.int32),
             pltpu.SMEM((devices,), jnp.int32),
-            pltpu.SemaphoreType.DMA((CHUNKS + 2,)),
+            pltpu.SemaphoreType.DMA((CHUNKS + 3,)),
         ],
         compiler_params=pltpu.CompilerParams(vmem_limit_bytes=52 << 20),
-    )(pltpu.with_memory_space_constraint(order, pltpu.HBM), pltpu.with_memory_space_constraint(runoff, pltpu.HBM), target,
-      pltpu.with_memory_space_constraint(weights, pltpu.HBM))
+    )(away(order), away(runoff), away(owners), me, away(weights))
 
 
 def coefficients(travel, weighting):
@@ -388,9 +412,9 @@
     sources, cells, reaches = weights.shape
     slots = 4
     targets = dest_device.reshape(devices, sources)
-    my_targets = lax.dynamic_slice(dest_device, (lax.axis_index("lat"), lon_index, 0, 0), (1, 1, sources, 1))
-    my_targets = my_targets.reshape(sources)
-    outgoing = map_sources(cell_order.reshape(sources, cells), runoff, my_targets, weights, devices, slots)
+    me = my_index.reshape(1).astype(jnp.int32)
+    outgoing = map_sources(cell_order.reshape(sources, cells), runoff, dest_device.reshape(devices * sources // 128, 128), me,
+                           weights, devices, slots)
     arrived = lax.all_to_all(outgoing.reshape(devices, slots * steps, reaches), ("lat", "lon"),
                              split_axis=0, concat_axis=0, tiled=True)
     arrived = arrived.reshape(devices * slots * steps, reaches)
@@ -403,9 +427,6 @@
 
     def near(x):
         return pltpu.with_memory_space_constraint(x, pltpu.VMEM)
-
-    def away(x):
-        return pltpu.with_memory_space_constraint(x, pltpu.HBM)
 
     far = pl.BlockSpec(memory_space=pltpu.HBM)
     blocks = initial_flow.shape[2]
@@ -433,7 +454,7 @@
         upstream_link.reshape(1, blocks),
         targets,
         dest_block.reshape(devices, sources),
-        my_index.reshape(1).astype(jnp.int32),
+        me,
     )
     lateral, notes = pl.pallas_call(
         functools.partial(lateral_kernel, steps, slots),

time: 87 us -> 84.1 us (0.967)
  Pallas kernels: 53.9 us -> 51.5 us
  local copies, waits for them, and re-layouts: 5.86 us -> 4.28 us
  waiting for transfers between devices: 10.8 us -> 11.7 us
    pallas_call x1, Pallas kernels: 15.9 us -> 13.7 us  [map_sources(): pl.pallas_call(functools.partial(map_kernel, slots), out_shape=jax.ShapeD...]
    unnamed x17, local copies, waits for them, and re-layouts: 5.18 us -> 4.28 us
  transfers between devices with their start and end apart: 2 -> 2, of which waited for: 2 -> 2; matrix products, arithmetic and copies ran while one was open for 0% -> 0% of each run, Pallas kernels for 38% -> 39%
where the time goes in v3:
time: 84.1 us; the launch traced here: 83.6 us
  Pallas kernels  51.5 us (61%)
  starting transfers between devices  15.8 us (19%)
  waiting for transfers between devices  11.7 us (14%)
  local copies, waits for them, and re-layouts  4.28 us (5%)
    pallas_call x1, Pallas kernels, body(): pl.pallas_call(functools.partial(prepare_kernel, steps, slots), out_shape...  26.7 us
    pallas_call x1, Pallas kernels, map_sources(): pl.pallas_call(functools.partial(map_kernel, slots), out_shape=jax.ShapeD...  13.7 us
    all_to_all x1, starting transfers between devices, body(): lax.all_to_all(outgoing.reshape(devices, slots * steps, reaches), ('lat',...  11.3 us
    all_to_all x1, waiting for transfers between devices, body(): lax.all_to_all(outgoing.reshape(devices, slots * steps, reaches), ('lat',...  9.26 us
    pallas_call x1, Pallas kernels, body(): pl.pallas_call(functools.partial(local_kernel, steps), out_shape=made(*pl...  6.07 us
    all_to_all x1, starting transfers between devices, body(): lax.all_to_all(notes, 'lon', split_axis=0, concat_axis=0, tiled=True)  4.49 us
    unnamed x17, local copies, waits for them, and re-layouts  4.28 us
    pallas_call x1, Pallas kernels, body(): pl.pallas_call(functools.partial(lateral_kernel, steps, slots), out_shape...  3.14 us
  transfers between devices with their start and end apart: 2, of which 2 were waited for; matrix products, arithmetic and copies ran while one was open for 0% of the time, Pallas kernels for 39%

profile of v3, /device:TPU:0, one launch (start us, length us, event | category | flops | bytes accessed | tf_op | source)
XLA Modules:
  0.0 83.6 jit_solution(15480665840541688627)
XLA Ops:
  0.0 0.0 copy-start.7
  0.0 0.0 copy-start.1
  0.0 0.0 copy-start.6
  0.0 13.7 %shard_map.109 = f32[6144,128]{1,0:T(8,128)} custom-call(s32[256,128]{1,0:T(8,128)} %bitcast.30, bf16[12,128,256]{2,1,0:T(8,128)(2,1)} %grid_ref.1, s32[256,128]{1,0:T(8,128)} %bitcast.29, s32[1]{0:T(128)} %bitcast.2.me_ref, bf16[256,128,128]{2,1,0:T(8,128)(2,1)} %bitcast.26), custom_call_target="tpu_custom_call" | custom-call | tf_op jit(solution)/shard_map/pallas_call | solution.py:186
  13.7 11.3 %all-to-all-start = ((f32[128,48,128]{2,1,0:T(8,128)}), f32[128,48,128]{2,1,0:T(8,128)S(1)}, u32[]{:S(2)}, u32[]{:S(2)}) async-start(f32[128,48,128]{2,1,0:T(8,128)} %bitcast.25), calls=%async_computation | async-start | bytes 6291456 | tf_op jit(solution)/shard_map/all_to_all | solution.py:418
  25.1 0.0 copy-done.7
  25.1 0.0 copy-done.1
  25.1 0.0 copy-done.6
  25.1 0.0 copy-start.2
  25.1 0.8 copy-done.2
  25.9 0.0 copy-start.3
  25.9 0.8 %copy-done.3 = f32[1,1,128,128]{3,2,1,0:T(8,128)S(1)} copy-done((f32[1,1,128,128]{3,2,1,0:T(8,128)S(1)}, f32[1,1,128,128]{3,2,1,0:T(8,128)}, u32[]{:S(2)}) %copy-start.3) | copy-done | bytes 65560
  26.8 0.0 copy-start.4
  26.8 0.8 %copy-done.4 = s32[1,1,128,128]{3,2,1,0:T(8,128)S(1)} copy-done((s32[1,1,128,128]{3,2,1,0:T(8,128)S(1)}, s32[1,1,128,128]{3,2,1,0:T(8,128)}, u32[]{:S(2)}) %copy-start.4) | copy-done | bytes 65560
  27.6 0.0 copy-start.5
  27.6 0.8 %copy-done.5 = f32[1,1,128,128]{3,2,1,0:T(8,128)S(1)} copy-done((f32[1,1,128,128]{3,2,1,0:T(8,128)S(1)}, f32[1,1,128,128]{3,2,1,0:T(8,128)}, u32[]{:S(2)}) %copy-start.5) | copy-done | bytes 65560
  28.5 26.7 %shard_map.110 = (f32[16384,128]{1,0:T(8,128)}, f32[12,128,128]{2,1,0:T(8,128)S(1)}, f32[12,128,128]{2,1,0:T(8,128)}, f32[4,128,128]{2,1,0:T(8,128)S(1)}, f32[40,128]{1,0:T(8,128)}) custom-call(f32[16384,128]{1,0:T(8,128)} %bitcast.27, f32[128,128]{1,0:T(8,128)S(1)} %bitcast.20, f32[128,128]{1,0:T(8,128)S(1)} %bitcast.21, s32[128,128]{1,0:T(8,128)S(1)} %bitcast.22, ...), custom_call_target="tpu_custom_call" | custom-call | flops 100663296 | bytes 20971520 | tf_op jit(solution)/shard_map/pallas_call | solution.py:439
  55.2 0.0 copy-start
  55.2 0.9 %copy-done = f32[12,128,128]{2,1,0:T(8,128)} copy-done((f32[12,128,128]{2,1,0:T(8,128)}, f32[12,128,128]{2,1,0:T(8,128)S(1)}, u32[]{:S(2)}) %copy-start) | copy-done | bytes 786456
  56.1 9.3 %all-to-all-done = f32[128,48,128]{2,1,0:T(8,128)S(1)} async-done(((f32[128,48,128]{2,1,0:T(8,128)}), f32[128,48,128]{2,1,0:T(8,128)S(1)}, u32[]{:S(2)}, u32[]{:S(2)}) %all-to-all-start) | async-done | bytes 3145760 | tf_op jit(solution)/shard_map/all_to_all | solution.py:418
  65.3 3.1 %shard_map.111 = (f32[12,128,128]{2,1,0:T(8,128)}, f32[16,32,128]{2,1,0:T(8,128)}) custom-call(f32[6144,128]{1,0:T(8,128)S(1)} %bitcast.17, f32[40,128]{1,0:T(8,128)} %get-tuple-element.12.far_note_ref, f32[12,128,128]{2,1,0:T(8,128)} %copy-done), custom_call_target="tpu_custom_call" | custom-call | tf_op jit(solution)/shard_map/pallas_call | solution.py:459
  68.5 4.5 %all-to-all-start.1 = ((f32[16,32,128]{2,1,0:T(8,128)}), f32[16,32,128]{2,1,0:T(8,128)S(1)}, u32[]{:S(2)}, u32[]{:S(2)}) async-start(f32[16,32,128]{2,1,0:T(8,128)} %get-tuple-element.14), calls=%async_computation.1 | async-start | bytes 524288 | tf_op jit(solution)/shard_map/all_to_all | solution.py:468
  73.0 6.1 %shard_map.112.flow_ref = f32[128,128]{1,0:T(8,128)S(1)} custom-call(f32[4,128,128]{2,1,0:T(8,128)S(1)} %get-tuple-element.15.terms_ref, f32[128,128,128]{2,1,0:T(8,128)} %bitcast.28, f32[12,128,128]{2,1,0:T(8,128)} %get-tuple-element.17.far_lateral_ref), custom_call_target="tpu_custom_call" | custom-call | flops 50331648 | bytes 8388608 | tf_op jit(solution)/shard_map/pallas_call | solution.py:469
  79.1 2.4 %all-to-all-done.1.notes_ref = f32[16,32,128]{2,1,0:T(8,128)S(1)} async-done(((f32[16,32,128]{2,1,0:T(8,128)}), f32[16,32,128]{2,1,0:T(8,128)S(1)}, u32[]{:S(2)}, u32[]{:S(2)}) %all-to-all-start.1) | async-done | bytes 262176 | tf_op jit(solution)/shard_map/all_to_all | solution.py:468
  81.5 1.9 %shard_map.113 = f32[128,128]{1,0:T(8,128)} custom-call(f32[16,32,128]{2,1,0:T(8,128)S(1)} %all-to-all-done.1.notes_ref, f32[128,128]{1,0:T(8,128)S(1)} %shard_map.112.flow_ref, f32[12,128,128]{2,1,0:T(8,128)} %get-tuple-element.18.far_heads_ref, s32[1]{0:T(128)} %bitcast.14.lon_ref), custom_call_target="tpu_custom_call" | custom-call | tf_op jit(solution)/shard_map/pallas_call | solution.py:479
  (1 shorter events, 0.0 us)
Async XLA Ops:
  0.0 25.1 %copy-start.7 = (s32[8,16,256,1]{2,3,1,0:T(1,128)S(1)}, s32[8,16,256,1]{2,3,1,0:T(1,128)}, u32[]{:S(2)}) copy-start(s32[8,16,256,1]{2,3,1,0:T(1,128)} %param.14) | copy-start | bytes 393220
  0.0 25.1 %copy-start.1 = (s32[8,16,256]{2,1,0:T(8,128)S(1)}, s32[8,16,256]{2,1,0:T(8,128)}, u32[]{:S(2)}) copy-start(s32[8,16,256]{2,1,0:T(8,128)} %param.15) | copy-start | bytes 393220
  0.0 25.1 %copy-start.6 = (s32[1,1,128]{2,1,0:T(1,128)S(1)}, s32[1,1,128]{2,1,0:T(1,128)}, u32[]{:S(2)}) copy-start(s32[1,1,128]{2,1,0:T(1,128)} %param.21) | copy-start | bytes 1540
  13.7 51.6 %all-to-all-start = ((f32[128,48,128]{2,1,0:T(8,128)}), f32[128,48,128]{2,1,0:T(8,128)S(1)}, u32[]{:S(2)}, u32[]{:S(2)}) async-start(f32[128,48,128]{2,1,0:T(8,128)} %bitcast.25), calls=%async_computation | async-start | bytes 6291456 | tf_op jit(solution)/shard_map/all_to_all | solution.py:418
  25.1 0.8 %copy-start.2 = (f32[1,1,128,128]{3,2,1,0:T(8,128)S(1)}, f32[1,1,128,128]{3,2,1,0:T(8,128)}, u32[]{:S(2)}) copy-start(f32[1,1,128,128]{3,2,1,0:T(8,128)} %param.17) | copy-start | bytes 196612
  25.9 0.8 %copy-start.3 = (f32[1,1,128,128]{3,2,1,0:T(8,128)S(1)}, f32[1,1,128,128]{3,2,1,0:T(8,128)}, u32[]{:S(2)}) copy-start(f32[1,1,128,128]{3,2,1,0:T(8,128)} %param.18) | copy-start | bytes 196612
  26.8 0.8 %copy-start.4 = (s32[1,1,128,128]{3,2,1,0:T(8,128)S(1)}, s32[1,1,128,128]{3,2,1,0:T(8,128)}, u32[]{:S(2)}) copy-start(s32[1,1,128,128]{3,2,1,0:T(8,128)} %param.19) | copy-start | bytes 196612
  27.6 0.8 %copy-start.5 = (f32[1,1,128,128]{3,2,1,0:T(8,128)S(1)}, f32[1,1,128,128]{3,2,1,0:T(8,128)}, u32[]{:S(2)}) copy-start(f32[1,1,128,128]{3,2,1,0:T(8,128)} %param.16) | copy-start | bytes 196612
  55.2 0.9 %copy-start = (f32[12,128,128]{2,1,0:T(8,128)}, f32[12,128,128]{2,1,0:T(8,128)S(1)}, u32[]{:S(2)}) copy-start(f32[12,128,128]{2,1,0:T(8,128)S(1)} %get-tuple-element.13.far_rows_ref) | copy-start | bytes 2359300
  68.5 13.0 %all-to-all-start.1 = ((f32[16,32,128]{2,1,0:T(8,128)}), f32[16,32,128]{2,1,0:T(8,128)S(1)}, u32[]{:S(2)}, u32[]{:S(2)}) async-start(f32[16,32,128]{2,1,0:T(8,128)} %get-tuple-element.14), calls=%async_computation.1 | async-start | bytes 524288 | tf_op jit(solution)/shard_map/all_to_all | solution.py:468

commit v4 on v3

--- a/solution.py
+++ b/solution.py
@@ -9,7 +9,7 @@
 substep_seconds = 300.0
 
 VREGS = 32
-CHUNKS = 4
+CHUNKS = 1
 TOGETHER = 6
 
 def gathered(x, index, axis):
@@ -155,7 +155,7 @@
 
     target_copy.wait()
     steps = 2 * planes
-    unroll = 64
+    unroll = 256
     for i in range(CHUNKS):
         fetch(i).wait()
         def group(g, carry):

time: 84.1 us -> 83.6 us (level)
  no operation moved by 1% of the time
where the time goes in v4:
time: 83.6 us; the launch traced here: 83.1 us
  Pallas kernels  51 us (61%)
  starting transfers between devices  15.8 us (19%)
  waiting for transfers between devices  11.7 us (14%)
  local copies, waits for them, and re-layouts  4.28 us (5%)
    pallas_call x1, Pallas kernels, body(): pl.pallas_call(functools.partial(prepare_kernel, steps, slots), out_shape...  26.7 us
    pallas_call x1, Pallas kernels, map_sources(): pl.pallas_call(functools.partial(map_kernel, slots), out_shape=jax.ShapeD...  13.2 us
    all_to_all x1, starting transfers between devices, body(): lax.all_to_all(outgoing.reshape(devices, slots * steps, reaches), ('lat',...  11.3 us
    all_to_all x1, waiting for transfers between devices, body(): lax.all_to_all(outgoing.reshape(devices, slots * steps, reaches), ('lat',...  9.26 us
    pallas_call x1, Pallas kernels, body(): pl.pallas_call(functools.partial(local_kernel, steps), out_shape=made(*pl...  6.07 us
    all_to_all x1, starting transfers between devices, body(): lax.all_to_all(notes, 'lon', split_axis=0, concat_axis=0, tiled=True)  4.49 us
    unnamed x17, local copies, waits for them, and re-layouts  4.28 us
    pallas_call x1, Pallas kernels, body(): pl.pallas_call(functools.partial(lateral_kernel, steps, slots), out_shape...  3.14 us
  transfers between devices with their start and end apart: 2, of which 2 were waited for; matrix products, arithmetic and copies ran while one was open for 0% of the time, Pallas kernels for 39%

profile of v4, /device:TPU:0, one launch (start us, length us, event | category | flops | bytes accessed | tf_op | source)
XLA Modules:
  0.0 83.1 jit_solution(9576298920360867682)
XLA Ops:
  0.0 0.0 copy-start.7
  0.0 0.0 copy-start.1
  0.0 0.0 copy-start.6
  0.0 13.2 %shard_map.109 = f32[6144,128]{1,0:T(8,128)} custom-call(s32[256,128]{1,0:T(8,128)} %bitcast.30, bf16[12,128,256]{2,1,0:T(8,128)(2,1)} %grid_ref.1, s32[256,128]{1,0:T(8,128)} %bitcast.29, s32[1]{0:T(128)} %bitcast.2.me_ref, bf16[256,128,128]{2,1,0:T(8,128)(2,1)} %bitcast.26), custom_call_target="tpu_custom_call" | custom-call | tf_op jit(solution)/shard_map/pallas_call | solution.py:186
  13.2 11.3 %all-to-all-start = ((f32[128,48,128]{2,1,0:T(8,128)}), f32[128,48,128]{2,1,0:T(8,128)S(1)}, u32[]{:S(2)}, u32[]{:S(2)}) async-start(f32[128,48,128]{2,1,0:T(8,128)} %bitcast.25), calls=%async_computation | async-start | bytes 6291456 | tf_op jit(solution)/shard_map/all_to_all | solution.py:418
  24.5 0.0 copy-done.7
  24.6 0.0 copy-done.1
  24.6 0.0 copy-done.6
  24.6 0.0 copy-start.2
  24.6 0.8 copy-done.2
  25.4 0.0 copy-start.3
  25.4 0.8 %copy-done.3 = f32[1,1,128,128]{3,2,1,0:T(8,128)S(1)} copy-done((f32[1,1,128,128]{3,2,1,0:T(8,128)S(1)}, f32[1,1,128,128]{3,2,1,0:T(8,128)}, u32[]{:S(2)}) %copy-start.3) | copy-done | bytes 65560
  26.3 0.0 copy-start.4
  26.3 0.8 %copy-done.4 = s32[1,1,128,128]{3,2,1,0:T(8,128)S(1)} copy-done((s32[1,1,128,128]{3,2,1,0:T(8,128)S(1)}, s32[1,1,128,128]{3,2,1,0:T(8,128)}, u32[]{:S(2)}) %copy-start.4) | copy-done | bytes 65560
  27.1 0.0 copy-start.5
  27.1 0.8 %copy-done.5 = f32[1,1,128,128]{3,2,1,0:T(8,128)S(1)} copy-done((f32[1,1,128,128]{3,2,1,0:T(8,128)S(1)}, f32[1,1,128,128]{3,2,1,0:T(8,128)}, u32[]{:S(2)}) %copy-start.5) | copy-done | bytes 65560
  28.0 26.7 %shard_map.110 = (f32[16384,128]{1,0:T(8,128)}, f32[12,128,128]{2,1,0:T(8,128)S(1)}, f32[12,128,128]{2,1,0:T(8,128)}, f32[4,128,128]{2,1,0:T(8,128)S(1)}, f32[40,128]{1,0:T(8,128)}) custom-call(f32[16384,128]{1,0:T(8,128)} %bitcast.27, f32[128,128]{1,0:T(8,128)S(1)} %bitcast.20, f32[128,128]{1,0:T(8,128)S(1)} %bitcast.21, s32[128,128]{1,0:T(8,128)S(1)} %bitcast.22, ...), custom_call_target="tpu_custom_call" | custom-call | flops 100663296 | bytes 20971520 | tf_op jit(solution)/shard_map/pallas_call | solution.py:439
  54.7 0.0 copy-start
  54.7 0.9 %copy-done = f32[12,128,128]{2,1,0:T(8,128)} copy-done((f32[12,128,128]{2,1,0:T(8,128)}, f32[12,128,128]{2,1,0:T(8,128)S(1)}, u32[]{:S(2)}) %copy-start) | copy-done | bytes 786456
  55.6 9.3 %all-to-all-done = f32[128,48,128]{2,1,0:T(8,128)S(1)} async-done(((f32[128,48,128]{2,1,0:T(8,128)}), f32[128,48,128]{2,1,0:T(8,128)S(1)}, u32[]{:S(2)}, u32[]{:S(2)}) %all-to-all-start) | async-done | bytes 3145760 | tf_op jit(solution)/shard_map/all_to_all | solution.py:418
  64.8 3.1 %shard_map.111 = (f32[12,128,128]{2,1,0:T(8,128)}, f32[16,32,128]{2,1,0:T(8,128)}) custom-call(f32[6144,128]{1,0:T(8,128)S(1)} %bitcast.17, f32[40,128]{1,0:T(8,128)} %get-tuple-element.12.far_note_ref, f32[12,128,128]{2,1,0:T(8,128)} %copy-done), custom_call_target="tpu_custom_call" | custom-call | tf_op jit(solution)/shard_map/pallas_call | solution.py:459
  68.0 4.5 %all-to-all-start.1 = ((f32[16,32,128]{2,1,0:T(8,128)}), f32[16,32,128]{2,1,0:T(8,128)S(1)}, u32[]{:S(2)}, u32[]{:S(2)}) async-start(f32[16,32,128]{2,1,0:T(8,128)} %get-tuple-element.14), calls=%async_computation.1 | async-start | bytes 524288 | tf_op jit(solution)/shard_map/all_to_all | solution.py:468
  72.5 6.1 %shard_map.112.flow_ref = f32[128,128]{1,0:T(8,128)S(1)} custom-call(f32[4,128,128]{2,1,0:T(8,128)S(1)} %get-tuple-element.15.terms_ref, f32[128,128,128]{2,1,0:T(8,128)} %bitcast.28, f32[12,128,128]{2,1,0:T(8,128)} %get-tuple-element.17.far_lateral_ref), custom_call_target="tpu_custom_call" | custom-call | flops 50331648 | bytes 8388608 | tf_op jit(solution)/shard_map/pallas_call | solution.py:469
  78.6 2.4 %all-to-all-done.1.notes_ref = f32[16,32,128]{2,1,0:T(8,128)S(1)} async-done(((f32[16,32,128]{2,1,0:T(8,128)}), f32[16,32,128]{2,1,0:T(8,128)S(1)}, u32[]{:S(2)}, u32[]{:S(2)}) %all-to-all-start.1) | async-done | bytes 262176 | tf_op jit(solution)/shard_map/all_to_all | solution.py:468
  81.0 1.9 %shard_map.113 = f32[128,128]{1,0:T(8,128)} custom-call(f32[16,32,128]{2,1,0:T(8,128)S(1)} %all-to-all-done.1.notes_ref, f32[128,128]{1,0:T(8,128)S(1)} %shard_map.112.flow_ref, f32[12,128,128]{2,1,0:T(8,128)} %get-tuple-element.18.far_heads_ref, s32[1]{0:T(128)} %bitcast.14.lon_ref), custom_call_target="tpu_custom_call" | custom-call | tf_op jit(solution)/shard_map/pallas_call | solution.py:479
  (1 shorter events, 0.0 us)
Async XLA Ops:
  0.0 24.5 %copy-start.7 = (s32[8,16,256,1]{2,3,1,0:T(1,128)S(1)}, s32[8,16,256,1]{2,3,1,0:T(1,128)}, u32[]{:S(2)}) copy-start(s32[8,16,256,1]{2,3,1,0:T(1,128)} %param.14) | copy-start | bytes 393220
  0.0 24.6 %copy-start.1 = (s32[8,16,256]{2,1,0:T(8,128)S(1)}, s32[8,16,256]{2,1,0:T(8,128)}, u32[]{:S(2)}) copy-start(s32[8,16,256]{2,1,0:T(8,128)} %param.15) | copy-start | bytes 393220
  0.0 24.6 %copy-start.6 = (s32[1,1,128]{2,1,0:T(1,128)S(1)}, s32[1,1,128]{2,1,0:T(1,128)}, u32[]{:S(2)}) copy-start(s32[1,1,128]{2,1,0:T(1,128)} %param.21) | copy-start | bytes 1540
  13.2 51.6 %all-to-all-start = ((f32[128,48,128]{2,1,0:T(8,128)}), f32[128,48,128]{2,1,0:T(8,128)S(1)}, u32[]{:S(2)}, u32[]{:S(2)}) async-start(f32[128,48,128]{2,1,0:T(8,128)} %bitcast.25), calls=%async_computation | async-start | bytes 6291456 | tf_op jit(solution)/shard_map/all_to_all | solution.py:418
  24.6 0.8 %copy-start.2 = (f32[1,1,128,128]{3,2,1,0:T(8,128)S(1)}, f32[1,1,128,128]{3,2,1,0:T(8,128)}, u32[]{:S(2)}) copy-start(f32[1,1,128,128]{3,2,1,0:T(8,128)} %param.17) | copy-start | bytes 196612
  25.4 0.8 %copy-start.3 = (f32[1,1,128,128]{3,2,1,0:T(8,128)S(1)}, f32[1,1,128,128]{3,2,1,0:T(8,128)}, u32[]{:S(2)}) copy-start(f32[1,1,128,128]{3,2,1,0:T(8,128)} %param.18) | copy-start | bytes 196612
  26.3 0.8 %copy-start.4 = (s32[1,1,128,128]{3,2,1,0:T(8,128)S(1)}, s32[1,1,128,128]{3,2,1,0:T(8,128)}, u32[]{:S(2)}) copy-start(s32[1,1,128,128]{3,2,1,0:T(8,128)} %param.19) | copy-start | bytes 196612
  27.1 0.8 %copy-start.5 = (f32[1,1,128,128]{3,2,1,0:T(8,128)S(1)}, f32[1,1,128,128]{3,2,1,0:T(8,128)}, u32[]{:S(2)}) copy-start(f32[1,1,128,128]{3,2,1,0:T(8,128)} %param.16) | copy-start | bytes 196612
  54.7 0.9 %copy-start = (f32[12,128,128]{2,1,0:T(8,128)}, f32[12,128,128]{2,1,0:T(8,128)S(1)}, u32[]{:S(2)}) copy-start(f32[12,128,128]{2,1,0:T(8,128)S(1)} %get-tuple-element.13.far_rows_ref) | copy-start | bytes 2359300
  68.0 13.0 %all-to-all-start.1 = ((f32[16,32,128]{2,1,0:T(8,128)}), f32[16,32,128]{2,1,0:T(8,128)S(1)}, u32[]{:S(2)}, u32[]{:S(2)}) async-start(f32[16,32,128]{2,1,0:T(8,128)} %get-tuple-element.14), calls=%async_computation.1 | async-start | bytes 524288 | tf_op jit(solution)/shard_map/all_to_all | solution.py:468
